TPU v7x, 128 devices: a whole 4x4x4 slice. The times are simulated.
128 devices in a mesh: row: 16 (over x, y), col: 8 (over z, core).
Axes of the slice: x: 4, y: 4, z: 4, core: 2. Of those that a mesh axis runs over, the one named last changes fastest.
Arguments:
- source_points: bfloat16 [65536, 1024], P('row'), may hold values from -8 to 8
- target_points: bfloat16 [32768, 1024], P('col', 'row'), may hold values from -8 to 8
- source_mass: float32 [65536], P('row'), may hold values from 0.25 to 4
- target_mass: float32 [32768], P('col'), may hold values from 0.25 to 4
- tile_index: int32 [256, 16], P('row', 'col'), may hold values from 0 to 15, as said below
- tile_count: int32 [256, 8], P('row', 'col'), may hold values from 1 to 2, as said below
Outputs:
- source_potential: float32 [65536], P('row')
- target_potential: float32 [32768], P('col')
Inputs may be any that keep to these rules, and one draw needn't show every extreme that they name: `tile_index`: within the 2 slots of one source tile and one index of col the target tiles are distinct; every target tile is named by a live slot of some source tile. `tile_count`: each index of row holds, for every index of col, a source tile with all 2 slots live.
All inputs are finite; a program needn't handle non-finite values.
Results may differ from a plain program's by a relative error of at most 0.0003.
Values may be sent and summed in bfloat16 or wider, within the bound.
A program may use at most 128 MiB of HBM per device.

v0:
```python
import math

import jax
import jax.numpy as jnp
from jax import lax
from jax.sharding import PartitionSpec as P

TILE = 256
ITERS = 3


masked_score = -1e30


def cost_terms(piece, source_points, tile_index):
    width = piece.shape[1]
    source_tiles = source_points.reshape(-1, TILE, width)
    target_tiles = piece.reshape(-1, TILE, width)
    chosen = target_tiles[tile_index]
    return jnp.einsum("rad,rkbd->rkab", source_tiles, chosen, preferred_element_type=jnp.float32)


def on_device(source_points, target_points, source_mass, target_mass, tile_index, tile_count):
    tiles_per_row = source_points.shape[0] // TILE
    col_tiles = target_points.shape[0] // TILE
    slot_count = tile_index.shape[1]
    scale = 1.0 / math.sqrt(source_points.shape[1])
    live = jnp.arange(slot_count)[None, :] < tile_count
    onehot = (tile_index[:, :, None] == jnp.arange(col_tiles)[None, None, :]) & live[:, :, None]
    log_source = jnp.log(source_mass).reshape(tiles_per_row, TILE)
    log_target = jnp.log(target_mass).reshape(col_tiles, TILE)
    target_pot = jnp.zeros((col_tiles, TILE), jnp.float32)
    source_pot = jnp.zeros((tiles_per_row, TILE), jnp.float32)
    for iteration in range(ITERS):
        cost = (
            cost_terms(
                lax.all_gather(target_points, "row", axis=1, tiled=True), source_points, tile_index
            )
            * scale
        )
        scores = cost + target_pot[tile_index][:, :, None, :]
        scores = jnp.where(live[:, :, None, None], scores, masked_score)
        row_top = jnp.max(scores, axis=(1, 3))
        highest = lax.pmax(row_top, "col")
        local_sum = jnp.sum(jnp.exp(scores - highest[:, None, :, None]), axis=(1, 3))
        total = lax.psum(local_sum, "col")
        source_pot = log_source - highest - jnp.log(total)
        columns = cost + source_pot[:, None, :, None]
        columns = jnp.where(live[:, :, None, None], columns, masked_score)
        slot_top = jnp.max(columns, axis=2)
        local_top = jnp.max(
            jnp.where(onehot[..., None], slot_top[:, :, None, :], masked_score), axis=(0, 1)
        )
        col_high = lax.pmax(local_top, "row")
        slot_ref = col_high[tile_index]
        sums = jnp.sum(jnp.exp(columns - slot_ref[:, :, None, :]), axis=2)
        col_sum = jnp.sum(jnp.where(onehot[..., None], sums[:, :, None, :], 0.0), axis=(0, 1))
        col_total = lax.psum(col_sum, "row")
        target_pot = log_target - col_high - jnp.log(col_total)
    return (source_pot.reshape(-1), target_pot.reshape(-1))


def solution(mesh):
    placed = (P("row", None), P("col", "row"), P("row"), P("col"), P("row", "col"), P("row", "col"))
    return jax.shard_map(
        on_device, mesh=mesh, in_specs=placed, out_specs=(P("row"), P("col")), check_vma=False
    )
```

profile of v0, /device:TPU:0, one launch (start us, length us, event | category | flops | bytes accessed | tf_op | source)
XLA Modules:
  0.0 747.4 jit_solution(9227641684370280702)
XLA Ops:
  7.2 0.0 all-gather.2.cloned.1.call-start
  7.2 0.7 all-gather.2.cloned.1.call-update
  7.9 0.8 copy.16
  8.7 0.7 compare_select_fusion
  9.3 0.1 copy.15
  9.4 0.1 reshape.101
  9.5 0.6 gather_fusion.1
  10.2 0.7 log.24
  10.9 0.7 log.25
  11.6 0.7 iota_compare_fusion
  12.4 0.1 compare_and_fusion
  12.5 70.8 %all-gather.2.cloned.1.call-done = bf16[4096,1024]{0,1:T(8,128)(2,1)} async-done(((bf16[4096,64]{0,1:T(8,128)(2,1)}), bf16[4096,1024]{0,1:T(8,128)(2,1)}) %all-gather.2.cloned.1.call-update) | async-done | bytes 8388624 | tf_op jit(solution)/shard_map/all_gather | solution.py:37
  83.2 12.0 %copy.14 = bf16[4096,1024]{1,0:T(8,128)(2,1)} copy(bf16[4096,1024]{0,1:T(8,128)(2,1)} %all-gather.2.cloned.1.call-done) | data formatting | bytes 16777216 | tf_op jit(solution)/shard_map/all_gather | solution.py:37
  95.2 10.6 %gather_fusion = bf16[32,256,1024]{2,1,0:T(8,128)(2,1)} fusion(bf16[16,256,1024]{2,1,0:T(8,128)(2,1)} %bitcast.57, s32[1024]{0:T(1024)S(1)} %pad_clamp_fusion), kind=kCustom, calls=%fused_computation | custom fusion | bytes 33554560 | tf_op jit(solution)/shard_map/gather | solution.py:19
  105.8 13.5 %bitcast_reduce_fusion.5 = (f32[16,256]{1,0:T(8,128)S(1)}, f32[16,2,256,256]{3,2,1,0:T(8,128)}) fusion(f32[16,2,256]{2,1,0:T(2,128)S(1)} %reshape.108, pred[16,2]{1,0:T(8,128)(4,1)S(1)} %iota_compare_fusion, bf16[16,2,256,1024]{3,2,1,0:T(8,128)(2,1)} %bitcast.58, bf16[16,256,1024,1]{2,1,3,0:T(8,128)(2,1)} %bitcast.63), kind=kOutput, calls=%fused_computation.28 | convolution fusion | flops 4303351808 | bytes 33603616 | tf_op jit(solution)/shard_map/rad,rkbd->rkab/dot_general | solution.py:20
  119.3 25.8 %pmax.42 = f32[16,256]{1,0:T(8,128)S(1)} all-reduce(f32[16,256]{1,0:T(8,128)S(1)} %get-tuple-element.2), channel_id=1, replica_groups=mesh['row'=16,'col'=8] {'col'}, use_global_device_ids=true, to_apply=%region_1.2 | all-reduce | flops 4096 | bytes 32768 | tf_op jit(solution)/shard_map/pmax | solution.py:44
  145.1 4.6 fusion.11
  149.7 23.6 %psum.42 = f32[16,256]{1,0:T(8,128)S(1)} all-reduce(f32[16,256]{1,0:T(8,128)S(1)} %fusion.11), channel_id=1, replica_groups=mesh['row'=16,'col'=8] {'col'}, use_global_device_ids=true, to_apply=%region_3.4 | all-reduce | flops 4096 | bytes 32768 | tf_op jit(solution)/shard_map/psum | solution.py:46
  173.3 4.7 bitcast_reduce_fusion.4
  178.0 0.1 select_reduce_fusion.5
  178.1 72.4 %pmax.43 = f32[16,256]{1,0:T(8,128)S(1)} all-reduce(f32[16,256]{1,0:T(8,128)S(1)} %select_reduce_fusion.5), channel_id=1, replica_groups=mesh['row'=16,'col'=8] {'row'}, use_global_device_ids=true, to_apply=%region_6.7 | all-reduce | flops 4096 | bytes 32768 | tf_op jit(solution)/shard_map/pmax | solution.py:54
  250.5 0.6 gather_fusion.2
  251.1 5.1 fusion.9
  256.2 0.1 select_reduce_fusion.4
  256.4 69.5 %psum.43 = f32[16,256]{1,0:T(8,128)S(1)} all-reduce(f32[16,256]{1,0:T(8,128)S(1)} %select_reduce_fusion.4), channel_id=1, replica_groups=mesh['row'=16,'col'=8] {'row'}, use_global_device_ids=true, to_apply=%region_9.10 | all-reduce | flops 4096 | bytes 32768 | tf_op jit(solution)/shard_map/psum | solution.py:58
  325.9 0.6 gather_fusion.3
  326.6 4.4 bitcast_reduce_fusion.3
  331.0 23.7 %pmax.44 = f32[16,256]{1,0:T(8,128)S(1)} all-reduce(f32[16,256]{1,0:T(8,128)S(1)} %bitcast_reduce_fusion.3), channel_id=1, replica_groups=mesh['row'=16,'col'=8] {'col'}, use_global_device_ids=true, to_apply=%region_11.12 | all-reduce | flops 4096 | bytes 32768 | tf_op jit(solution)/shard_map/pmax | solution.py:44
  354.7 4.6 fusion.7
  359.4 23.6 %psum.44 = f32[16,256]{1,0:T(8,128)S(1)} all-reduce(f32[16,256]{1,0:T(8,128)S(1)} %fusion.7), channel_id=1, replica_groups=mesh['row'=16,'col'=8] {'col'}, use_global_device_ids=true, to_apply=%region_13.14 | all-reduce | flops 4096 | bytes 32768 | tf_op jit(solution)/shard_map/psum | solution.py:46
  382.9 4.7 bitcast_reduce_fusion.2
  387.6 0.1 select_reduce_fusion.3
  387.8 69.5 %pmax.45 = f32[16,256]{1,0:T(8,128)S(1)} all-reduce(f32[16,256]{1,0:T(8,128)S(1)} %select_reduce_fusion.3), channel_id=1, replica_groups=mesh['row'=16,'col'=8] {'row'}, use_global_device_ids=true, to_apply=%region_16.17 | all-reduce | flops 4096 | bytes 32768 | tf_op jit(solution)/shard_map/pmax | solution.py:54
  457.3 0.6 gather_fusion.4
  457.9 5.1 fusion.5
  463.1 0.1 select_reduce_fusion.2
  463.2 69.5 %psum.45 = f32[16,256]{1,0:T(8,128)S(1)} all-reduce(f32[16,256]{1,0:T(8,128)S(1)} %select_reduce_fusion.2), channel_id=1, replica_groups=mesh['row'=16,'col'=8] {'row'}, use_global_device_ids=true, to_apply=%region_19.20 | all-reduce | flops 4096 | bytes 32768 | tf_op jit(solution)/shard_map/psum | solution.py:58
  532.7 0.6 gather_fusion.5
  533.4 4.4 bitcast_reduce_fusion.1
  537.8 23.6 %pmax.46 = f32[16,256]{1,0:T(8,128)S(1)} all-reduce(f32[16,256]{1,0:T(8,128)S(1)} %bitcast_reduce_fusion.1), channel_id=1, replica_groups=mesh['row'=16,'col'=8] {'col'}, use_global_device_ids=true, to_apply=%region_21.22 | all-reduce | flops 4096 | bytes 32768 | tf_op jit(solution)/shard_map/pmax | solution.py:44
  561.4 4.6 fusion.3
  566.0 23.6 %psum.46 = f32[16,256]{1,0:T(8,128)S(1)} all-reduce(f32[16,256]{1,0:T(8,128)S(1)} %fusion.3), channel_id=1, replica_groups=mesh['row'=16,'col'=8] {'col'}, use_global_device_ids=true, to_apply=%region_23.24 | all-reduce | flops 4096 | bytes 32768 | tf_op jit(solution)/shard_map/psum | solution.py:46
  589.6 4.7 bitcast_reduce_fusion
  594.2 0.1 select_reduce_fusion.1
  594.4 69.5 %pmax.47 = f32[16,256]{1,0:T(8,128)S(1)} all-reduce(f32[16,256]{1,0:T(8,128)S(1)} %select_reduce_fusion.1), channel_id=1, replica_groups=mesh['row'=16,'col'=8] {'row'}, use_global_device_ids=true, to_apply=%region_26.27 | all-reduce | flops 4096 | bytes 32768 | tf_op jit(solution)/shard_map/pmax | solution.py:54
  663.9 0.6 gather_fusion.6
  664.6 5.1 fusion.1
  669.7 0.1 select_reduce_fusion
  669.8 69.5 %psum.47 = f32[16,256]{1,0:T(8,128)S(1)} all-reduce(f32[16,256]{1,0:T(8,128)S(1)} %select_reduce_fusion), channel_id=1, replica_groups=mesh['row'=16,'col'=8] {'row'}, use_global_device_ids=true, to_apply=%region_29.30 | all-reduce | flops 4096 | bytes 32768 | tf_op jit(solution)/shard_map/psum | solution.py:58
  739.4 0.6 copy.19
  740.0 0.6 copy.18
  (16 shorter events, 0.2 us)
Async XLA Ops:
  7.2 76.1 %all-gather.2.cloned.1.call-start = ((), (), s32[]{:S(2)}) async-start(), calls=%async_computation | async-start | bytes 8912896 | tf_op jit(solution)/shard_map/all_gather | solution.py:37
Sparse Core Ops, SparseCore 0:
  10.1 73.0 all-gather.1
where the time goes:
time: 748 us; the launch traced here: 747 us
  blocking collectives  564 us (75%)
  waiting for transfers between devices  71.4 us (10%)
  other arithmetic  54.5 us (7%)
  local copies, waits for them, and re-layouts  30 us (4%)
  between operations  14.3 us (2%)
  matrix products  13.5 us (2%)
    pmax x3, blocking collectives, on_device(): col_high = lax.pmax(local_top, 'row')  211 us
    psum x3, blocking collectives, on_device(): col_total = lax.psum(col_sum, 'row')  209 us
    pmax x3, blocking collectives, on_device(): highest = lax.pmax(row_top, 'col')  73.1 us
    all_gather x1, waiting for transfers between devices, on_device(): lax.all_gather(target_points, 'row', axis=1, tiled=True)  70.8 us
    psum x3, blocking collectives, on_device(): total = lax.psum(local_sum, 'col')  70.7 us
    reduce_sum x3, other arithmetic, on_device(): sums = jnp.sum(jnp.exp(columns - slot_ref[:, :, None, :]), axis=2)  15.4 us
  transfers between devices with their start and end apart: 1, of which 1 were waited for; matrix products, arithmetic and copies ran while one was open for 1% of the time, Pallas kernels for 0%

commit v1 on v0

v1 whole, which is shorter than its diff:
```python
import functools
import math

import jax
import jax.numpy as jnp
from jax import lax
from jax.experimental import pallas as pl
from jax.experimental.pallas import tpu as pltpu
from jax.sharding import PartitionSpec as P

TILE = 256
ITERS = 3
LOG2E = 1.4426950408889634
LN2 = 0.6931471805599453
NEG = -1e30
MESH = pl.DeviceIdType.MESH
HALF = 2048
QUART = 1024


def log2(v):
    return jnp.log(v) * LOG2E


def kernel(
    nx, ny, ncol, parts,
    ti, tv, tc, sp, tp, sm, tm, f_out, g_out,
    X, T0, T1, T2, T3, S, ST, GB, FB, MS, QS, FV, RC, RR, IV,
    lsem, gs, gr, cs, cr, rs, rr,
):
    T = (T0, T1, T2, T3)
    row = lax.axis_index("row")
    col = lax.axis_index("col")
    nrow = nx * ny
    x, y = row // ny, lax.rem(row, ny)

    def at(dx, dy):
        return (lax.rem(x + dx + nx, nx) * ny + lax.rem(y + dy + ny, ny), col)

    def row_peer(k):
        return (lax.rem(row + k, nrow), col)

    def col_peer(k):
        return (row, lax.rem(col + k, ncol))

    load_x = pltpu.make_async_copy(sp, X, lsem.at[0])
    load_x.start()

    barrier = pltpu.get_barrier_semaphore()
    for k in range(1, nrow):
        pl.semaphore_signal(barrier, inc=1, device_id=row_peer(k), device_id_type=MESH)
    for k in range(1, ncol):
        pl.semaphore_signal(barrier, inc=1, device_id=col_peer(k), device_id_type=MESH)
    pl.semaphore_wait(barrier, nrow + ncol - 2)

    sent = []

    def rows(dy):
        return pl.ds(pl.multiple_of(lax.rem(y + dy + ny, ny) * 64, 64), 64)

    def send(src, dst, to):
        k = len(sent)
        c = pltpu.make_async_remote_copy(
            src_ref=src, dst_ref=dst, send_sem=gs.at[k], recv_sem=gr.at[k],
            device_id=to, device_id_type=MESH,
        )
        c.start()
        sent.append(c)
        return c

    A, B = pl.ds(0, HALF), pl.ds(HALF, HALF)
    A0, A1 = pl.ds(0, QUART), pl.ds(QUART, QUART)
    B0, B1 = pl.ds(HALF, QUART), pl.ds(HALF + QUART, QUART)

    def own(part):
        return tp.at[:, part]

    def along_y(src, d, part, dy):
        up = send(src, T[d].at[rows(dy), part], at(0, 1))
        down = send(src, T[d].at[rows(dy), part], at(0, -1))
        return up, down

    def along_x(src, part, dy):
        up = send(src, T[3].at[rows(dy), part], at(1, 0))
        down = send(src, T[1].at[rows(dy), part], at(-1, 0))
        return up, down

    def forward_y(pair, d, low, high):
        pair[0].wait_recv()
        a = send(T[d].at[rows(-1), low], T[d].at[rows(-1), low], at(0, 1))
        pair[1].wait_recv()
        b = send(T[d].at[rows(1), high], T[d].at[rows(1), high], at(0, -1))
        return a, b

    def forward_x(pair, dy, low, high):
        pair[0].wait_recv()
        a = send(T[3].at[rows(dy), low], T[2].at[rows(dy), low], at(1, 0))
        pair[1].wait_recv()
        b = send(T[1].at[rows(dy), high], T[2].at[rows(dy), high], at(-1, 0))
        return a, b

    def done(*pairs):
        for pair in pairs:
            for c in pair:
                c.wait_recv()

    scale = LOG2E / math.sqrt(sp.shape[1])

    def scores(d):
        cols = pl.ds(pl.multiple_of(lax.rem(x + d, nx) * 256, 256), 256)

        def body(t, carry):
            left = X[pl.ds(pl.multiple_of(t * TILE, TILE), TILE), cols]
            for s in range(2):
                u = ti[s, t]
                right = T[d][:, pl.ds(u * TILE, TILE)]
                new = jnp.dot(left, right, preferred_element_type=jnp.float32)
                p = s * 16 + t
                if d == 0:
                    S[p] = new
                elif d == 2:
                    new = (S[p] + new) * scale
                    S[p] = new
                    ST[p] = new.T
                else:
                    S[p] = S[p] + new
            return carry

        lax.fori_loop(0, 16, body, 0)

    if parts[0]:
        a1 = along_x(own(A), A, 0)
        b1 = along_y(own(B), 0, B, 0)
        ay0 = along_y(own(A), 0, A, 0)
        bx0 = along_x(own(B), B, 0)
    keep = pltpu.make_async_copy(tp, T[0].at[rows(0), :], lsem.at[1])
    keep.start()

    GB[...] = jnp.zeros_like(GB)
    diagonal = lax.broadcasted_iota(jnp.int32, (16, 16), 0) == lax.broadcasted_iota(jnp.int32, (16, 16), 1)
    for s in range(2):
        name = jnp.where(tc[...] > s, tv[s:s + 1, :], -1).astype(jnp.float32)
        down = jnp.sum(jnp.where(diagonal, jnp.broadcast_to(name, (16, 16)), 0.0), axis=1, keepdims=True)
        IV[s * 16:(s + 1) * 16, :] = jnp.broadcast_to(down, (16, 128))

    if parts[0]:
        a2 = forward_x(a1, 0, A0, A1)
        ay3 = along_y(T[3].at[rows(0), A], 3, A, 0)
        ay1 = along_y(T[1].at[rows(0), A], 1, A, 0)
        b2 = forward_y(b1, 0, B0, B1)
        bx3 = along_x(T[0].at[rows(-1), B], B, -1)
        bx1 = along_x(T[0].at[rows(1), B], B, 1)
        fay0 = forward_y(ay0, 0, A0, A1)
        fbx0 = forward_x(bx0, 0, B0, B1)
        done(a2)
        ay2 = along_y(T[2].at[rows(0), A], 2, A, 0)
        done(b2)
        bx2 = along_x(T[0].at[rows(2), B], B, 2)
        done(fay0)
    keep.wait()
    load_x.wait()
    if parts[1]:
        scores(0)
    if parts[0]:
        fay3 = forward_y(ay3, 3, A0, A1)
        fay1 = forward_y(ay1, 1, A0, A1)
        fbx3 = forward_x(bx3, -1, B0, B1)
        fbx1 = forward_x(bx1, 1, B0, B1)
        fay2 = forward_y(ay2, 2, A0, A1)
        fbx2 = forward_x(bx2, 2, B0, B1)
        done(fay3, fay1)
    if parts[1]:
        scores(3)
        scores(1)
    if parts[0]:
        done(fbx0, fbx3, fbx1, fay2, fbx2)
    if parts[1]:
        scores(2)

    def each_tile(src, add):
        def body(t, carry):
            for s in range(2):
                p = s * 16 + t
                for h in range(2):
                    r = src[p, :, h * 128:(h + 1) * 128] + add(s, t)
                    top = jnp.max(r, axis=0, keepdims=True)
                    total = jnp.sum(jnp.exp2(r - top), axis=0, keepdims=True)
                    MS[h, pl.ds(p, 1), :] = top
                    QS[h, pl.ds(p, 1), :] = total
            return carry

        lax.fori_loop(0, 16, body, 0)

    def spread(dst):
        def body(t, carry):
            for h in range(2):
                v = jnp.broadcast_to(FV[h, pl.ds(t, 1), :], (128, 128))
                dst[t, h * 128:(h + 1) * 128, :] = v.T
            return carry

        lax.fori_loop(0, 16, body, 0)

    def merged(got):
        top = jnp.max(got, axis=0)
        return top + log2(jnp.sum(jnp.exp2(got - top[None]), axis=0))

    def exchange(buf, it, me, n, peer, ss, rsem):
        copies = []
        for k in range(1, n):
            c = pltpu.make_async_remote_copy(
                src_ref=buf.at[it, me], dst_ref=buf.at[it, me],
                send_sem=ss.at[it, k], recv_sem=rsem.at[it, k],
                device_id=peer(k), device_id_type=MESH,
            )
            c.start()
            copies.append(c)
        for c in copies:
            c.wait()

    def iteration(it, carry):
        if parts[2]:
            each_tile(ST, lambda s, t: GB[ti[s, t]])
        for h in range(2):
            one = jnp.where(IV[...] < 0.0, NEG, MS[h] + log2(QS[h]))
            a, b = one[:16], one[16:]
            top = jnp.maximum(a, b)
            RC[it, col, h] = top + log2(jnp.exp2(a - top) + jnp.exp2(b - top))
        if parts[3]:
            exchange(RC, it, col, ncol, col_peer, cs, cr)
        for h in range(2):
            log_mass = log2(sm[pl.ds(h, 16, stride=2), :])
            f = log_mass - merged(RC[it, :, h])
            FV[h] = f
            f_out[pl.ds(h, 16, stride=2), :] = f
        if parts[2]:
            spread(FB)
            each_tile(S, lambda s, t: FB[t])
        for h in range(2):
            one = MS[h] + log2(QS[h])
            for u in range(16):
                named = IV[...] == float(u)
                top = jnp.max(jnp.where(named, one, NEG), axis=0, keepdims=True)
                total = jnp.sum(jnp.where(named, jnp.exp2(one - top), 0.0), axis=0, keepdims=True)
                RR[it, row, h, pl.ds(u, 1), :] = top + log2(jnp.maximum(total, 1e-30))
        if parts[4]:
            exchange(RR, it, row, nrow, row_peer, rs, rr)
        for h in range(2):
            log_mass = log2(tm[pl.ds(h, 16, stride=2), :])
            g = log_mass - merged(RR[it, :, h])
            FV[h] = g
            g_out[pl.ds(h, 16, stride=2), :] = g
        if parts[2]:
            spread(GB)
        return carry

    lax.fori_loop(0, ITERS, iteration, 0)
    for c in sent:
        c.wait_send()


def build(mesh, parts):
    ncol = mesh.shape["col"]
    nrow = mesh.shape["row"]
    nx = ny = math.isqrt(nrow)

    def on_device(source_points, target_points, source_mass, target_mass, tile_index, tile_count):
        n, d = source_points.shape
        m = target_points.shape[0]
        vmem = pl.BlockSpec(memory_space=pltpu.VMEM)
        smem = pl.BlockSpec(memory_space=pltpu.SMEM)
        hbm = pl.BlockSpec(memory_space=pl.ANY)
        f32 = jnp.float32
        f, g = pl.pallas_call(
            functools.partial(kernel, nx, ny, ncol, parts),
            out_shape=(
                jax.ShapeDtypeStruct((n // 128, 128), f32),
                jax.ShapeDtypeStruct((m // 128, 128), f32),
            ),
            in_specs=[smem, vmem, vmem, hbm, hbm, vmem, vmem],
            out_specs=(vmem, vmem),
            scratch_shapes=[
                pltpu.VMEM((n, d), jnp.bfloat16),
                *[pltpu.VMEM((256, m), jnp.bfloat16) for _ in range(4)],
                pltpu.VMEM((32, TILE, TILE), f32),
                pltpu.VMEM((32, TILE, TILE), f32),
                pltpu.VMEM((16, TILE, 128), f32),
                pltpu.VMEM((16, TILE, 128), f32),
                pltpu.VMEM((2, 32, 128), f32),
                pltpu.VMEM((2, 32, 128), f32),
                pltpu.VMEM((2, 16, 128), f32),
                pltpu.VMEM((ITERS, ncol, 2, 16, 128), f32),
                pltpu.VMEM((ITERS, nrow, 2, 16, 128), f32),
                pltpu.VMEM((32, 128), f32),
                pltpu.SemaphoreType.DMA((2,)),
                pltpu.SemaphoreType.DMA((40,)),
                pltpu.SemaphoreType.DMA((40,)),
                pltpu.SemaphoreType.DMA((ITERS, ncol)),
                pltpu.SemaphoreType.DMA((ITERS, ncol)),
                pltpu.SemaphoreType.DMA((ITERS, nrow)),
                pltpu.SemaphoreType.DMA((ITERS, nrow)),
            ],
            compiler_params=pltpu.CompilerParams(
                collective_id=0, has_side_effects=True, vmem_limit_bytes=60 * 2**20
            ),
        )(
            tile_index.T, tile_index.T, tile_count.T, source_points, target_points.T,
            source_mass.reshape(-1, 128), target_mass.reshape(-1, 128),
        )
        return (f * LN2).reshape(-1), (g * LN2).reshape(-1)

    placed = (P("row", None), P("col", "row"), P("row"), P("col"), P("row", "col"), P("row", "col"))
    return jax.shard_map(
        on_device, mesh=mesh, in_specs=placed, out_specs=(P("row"), P("col")), check_vma=False
    )


def solution(mesh):
    return build(mesh, (True,) * 5)
```

time: 748 us -> 125 us (0.17)
  blocking collectives: 564 us -> 0 us
  Pallas kernels: 0 us -> 122 us
  waiting for transfers between devices: 71.4 us -> 0 us
  other arithmetic: 54.5 us -> 1.35 us
  local copies, waits for them, and re-layouts: 30 us -> 0 us
  between operations: 14.3 us -> 0.64 us
  matrix products: 13.5 us -> 0 us
    pmax x6 -> x0, blocking collectives: 284 us -> none  [the longest x3 211 us: on_device(): col_high = lax.pmax(local_top, 'row')]
    psum x6 -> x0, blocking collectives: 279 us -> none  [the longest x3 209 us: on_device(): col_total = lax.psum(col_sum, 'row')]
    pallas_call x0 -> x1, Pallas kernels: none -> 122 us  [on_device(): pl.pallas_call(functools.partial(kernel, nx, ny, ncol, parts), out_shape=...]
    all_gather x1 -> x0, waiting for transfers between devices: 70.8 us -> none  [on_device(): lax.all_gather(target_points, 'row', axis=1, tiled=True)]
    reduce_sum x9 -> x0, other arithmetic: 29.7 us -> none  [the longest x3 15.4 us: on_device(): sums = jnp.sum(jnp.exp(columns - slot_ref[:, :, None, :]), axis=2)]
    reduce_max x8 -> x0, other arithmetic: 23.2 us -> none  [the longest x3 14 us: on_device(): slot_top = jnp.max(columns, axis=2)]
    gather x13 -> x0, local copies, waits for them, and re-layouts: 14.4 us -> none  [the longest x1 10.6 us: cost_terms(): chosen = target_tiles[tile_index]]
    dot_general x1 -> x0, matrix products: 13.5 us -> none  [cost_terms(): jnp.einsum('rad,rkbd->rkab', source_tiles, chosen, preferred_element_type...]
  transfers between devices with their start and end apart: 1 -> 0, of which waited for: 1 -> 0; matrix products, arithmetic and copies ran while one was open for 1% -> 0% of each run, Pallas kernels for 0% -> 0%
where the time goes in v1:
time: 125 us; the launch traced here: 124 us
  Pallas kernels  122 us (98%)
  other arithmetic  1.35 us (1%)
    pallas_call x1, Pallas kernels, on_device(): pl.pallas_call(functools.partial(kernel, nx, ny, ncol, parts), out_shape=...  122 us

profile of v1, /device:TPU:0, one launch (start us, length us, event | category | flops | bytes accessed | tf_op | source)
XLA Modules:
  0.0 124.2 jit_solution(5601972836073960301)
XLA Ops:
  0.6 122.2 %shard_map.77 = (f32[32,128]{1,0:T(8,128)}, f32[32,128]{1,0:T(8,128)}) custom-call(s32[2,16]{1,0:T(2,128)} %bitcast.12, s32[2,16]{1,0:T(2,128)} %bitcast.13, s32[1,16]{1,0:T(1,128)} %bitcast.14, bf16[4096,1024]{1,0:T(8,128)(2,1)} %sp.1, bf16[64,4096]{1,0:T(8,128)(2,1)} %bitcast.9, f32[32,128]{1,0:T(8,128)} %bitcast.10, f32[32,128]{1,0:T(8,128)} %bitcast.11), custom_call_target="tpu_custom_call" | custom-call | tf_op jit(solution)/shard_map/pallas_call | solution.py:273
  122.8 1.4 %multiply_bitcast_fusion = (f32[4096]{0:T(1024)}, f32[4096]{0:T(1024)}) fusion(f32[32,128]{1,0:T(8,128)} %get-tuple-element.5, f32[32,128]{1,0:T(8,128)} %get-tuple-element.4), kind=kLoop, calls=%fused_computation | loop fusion | flops 8192 | bytes 65536 | tf_op jit(solution)/shard_map/reshape | solution.py:309

commit v2 on v1

v2 whole, which is shorter than its diff:
```python
import functools
import math

import jax
import jax.numpy as jnp
from jax import lax
from jax.experimental import pallas as pl
from jax.experimental.pallas import tpu as pltpu
from jax.sharding import PartitionSpec as P

TILE = 256
ITERS = 3
LOG2E = 1.4426950408889634
LN2 = 0.6931471805599453
NEG = -1e30
MESH = pl.DeviceIdType.MESH
HALF = 2048
QUART = 1024


def log2(v):
    return jnp.log(v) * LOG2E


def kernel(
    nx, ny, ncol, parts,
    ti, tc, tv, cv, sp, tp, sm, tm, f_out, g_out,
    X, T0, T1, T2, T3, S, MB, FB, MS, QS, M8, W8, FV, GV, UV, RC, RR, IV,
    lsem, gs, gr, cr, rs, es,
):
    T = (T0, T1, T2, T3)
    row = lax.axis_index("row")
    col = lax.axis_index("col")
    nrow = nx * ny
    x, y = row // ny, lax.rem(row, ny)

    def at(dx, dy):
        return (lax.rem(x + dx + nx, nx) * ny + lax.rem(y + dy + ny, ny), col)

    def row_peer(k):
        return (lax.rem(row + k, nrow), col)

    def col_peer(k):
        return (row, lax.rem(col + k, ncol))

    load_x = pltpu.make_async_copy(sp, X, lsem.at[0])
    load_x.start()

    barrier = pltpu.get_barrier_semaphore()
    for k in range(1, nrow):
        pl.semaphore_signal(barrier, inc=1, device_id=row_peer(k), device_id_type=MESH)
    for k in range(1, ncol):
        pl.semaphore_signal(barrier, inc=1, device_id=col_peer(k), device_id_type=MESH)
    pl.semaphore_wait(barrier, nrow + ncol - 2)

    used = []

    def rows(dy):
        return pl.ds(pl.multiple_of(lax.rem(y + dy + ny, ny) * 64, 64), 64)

    steps = {0: (1, 0), 1: (-1, 0), 2: (0, 1), 3: (0, -1)}

    def fresh():
        used.append(0)
        return len(used) - 1

    def send(src, dst, link, k=None):
        k = fresh() if k is None else k
        c = pltpu.make_async_remote_copy(
            src_ref=src, dst_ref=dst, send_sem=gs.at[link], recv_sem=gr.at[k],
            device_id=at(*steps[link]), device_id_type=MESH,
        )
        c.start()
        return c

    A, B = pl.ds(0, HALF), pl.ds(HALF, HALF)
    A0, A1 = pl.ds(0, QUART), pl.ds(QUART, QUART)
    B0, B1 = pl.ds(HALF, QUART), pl.ds(HALF + QUART, QUART)

    def own(part):
        return tp.at[:, part]

    def along_y(src, d, part, dy):
        return tuple(send(src, T[d].at[rows(dy), part], link) for link in (2, 3))

    def along_x(src, part, dy):
        return (
            send(src, T[3].at[rows(dy), part], 0),
            send(src, T[1].at[rows(dy), part], 1),
        )

    def forward_y(pair, d, low, high):
        k = fresh()
        pair[0].wait_recv()
        send(T[d].at[rows(-1), low], T[d].at[rows(-1), low], 2, k)
        pair[1].wait_recv()
        send(T[d].at[rows(1), high], T[d].at[rows(1), high], 3, k)
        return k

    def forward_x(pair, dy, low, high):
        k = fresh()
        pair[0].wait_recv()
        send(T[3].at[rows(dy), low], T[2].at[rows(dy), low], 0, k)
        pair[1].wait_recv()
        send(T[1].at[rows(dy), high], T[2].at[rows(dy), high], 1, k)
        return k

    def done(*sems):
        for k in sems:
            whole = T[0].at[rows(0), A]
            pltpu.make_async_copy(whole, whole, gr.at[k]).wait()

    scale = LOG2E / math.sqrt(sp.shape[1])
    wide = (32, 8, 128)
    diagonal = lax.broadcasted_iota(jnp.int32, (128, 128), 0) == lax.broadcasted_iota(jnp.int32, (128, 128), 1)

    def to_row(v):
        return jnp.sum(jnp.where(diagonal, jnp.broadcast_to(v, (128, 128)), 0.0), axis=0, keepdims=True)

    def product(d, t, s):
        cols = pl.ds(pl.multiple_of(lax.rem(x + d, nx) * 256, 256), 256)
        left = X[pl.ds(pl.multiple_of(t * TILE, TILE), TILE), cols]
        right = T[d][:, pl.ds(ti[s, t] * TILE, TILE)]
        return jnp.dot(left, right, preferred_element_type=jnp.float32) * scale

    def scores(d):
        def body(t, carry):
            for s in range(2):
                p = s * 16 + t
                new = product(d, t, s)
                S[p] = new if d == 0 else S[p] + new
            return carry

        lax.fori_loop(0, 16, body, 0)

    def idle(t):
        return (tc[0, t].astype(jnp.float32) - 2.0) * 1e30

    if parts[0]:
        a1 = along_x(own(A), A, 0)
        b1 = along_y(own(B), 0, B, 0)
        ay0 = along_y(own(A), 0, A, 0)
        bx0 = along_x(own(B), B, 0)
    keep = pltpu.make_async_copy(tp, T[0].at[rows(0), :], lsem.at[1])
    keep.start()

    small = lax.broadcasted_iota(jnp.int32, (16, 16), 0) == lax.broadcasted_iota(jnp.int32, (16, 16), 1)
    for s in range(2):
        name = jnp.where(cv[...] > s, tv[s:s + 1, :], -1).astype(jnp.float32)
        down = jnp.sum(jnp.where(small, jnp.broadcast_to(name, (16, 16)), 0.0), axis=1, keepdims=True)
        IV[s * 16:(s + 1) * 16, :] = jnp.broadcast_to(down, (16, 128))

    if parts[0]:
        a2 = forward_x(a1, 0, A0, A1)
        ay3 = along_y(T[3].at[rows(0), A], 3, A, 0)
        ay1 = along_y(T[1].at[rows(0), A], 1, A, 0)
        b2 = forward_y(b1, 0, B0, B1)
        bx3 = along_x(T[0].at[rows(-1), B], B, -1)
        bx1 = along_x(T[0].at[rows(1), B], B, 1)
        fay0 = forward_y(ay0, 0, A0, A1)
        fbx0 = forward_x(bx0, 0, B0, B1)
        done(a2)
        ay2 = along_y(T[2].at[rows(0), A], 2, A, 0)
        done(b2)
        bx2 = along_x(T[0].at[rows(2), B], B, 2)
        done(fay0)
    keep.wait()
    load_x.wait()
    if parts[1]:
        scores(0)
    if parts[0]:
        fay3 = forward_y(ay3, 3, A0, A1)
        fay1 = forward_y(ay1, 1, A0, A1)
        fbx3 = forward_x(bx3, -1, B0, B1)
        fbx1 = forward_x(bx1, 1, B0, B1)
        fay2 = forward_y(ay2, 2, A0, A1)
        fbx2 = forward_x(bx2, 2, B0, B1)
        done(fay3, fay1)
    if parts[1]:
        scores(3)
        scores(1)
    if parts[0]:
        done(fbx0, fbx3, fbx1, fay2, fbx2)

    def finish(t):
        tops = []
        for s in range(2):
            p = s * 16 + t
            r = S[p] + product(2, t, s)
            S[p] = r
            tops.append(jnp.maximum(r[:, :128], r[:, 128:]))
        top = jnp.max(jnp.maximum(tops[0], tops[1] + idle(t)), axis=1, keepdims=True)
        MB[lax.rem(t, 2)] = jnp.broadcast_to(top, (TILE, 128))

    def row_logs(t):
        top = MB[lax.rem(t, 2)]
        total = jnp.zeros((TILE, 128), jnp.float32)
        for s in range(2):
            shift = top if s == 0 else top - idle(t)
            for h in range(2):
                total += jnp.exp2(S[s * 16 + t, :, h * 128:(h + 1) * 128] - shift)
        value = top[:, :1] + log2(jnp.sum(total, axis=1, keepdims=True))
        for h in range(2):
            RC[0, col, h, pl.ds(t, 1), :] = to_row(value[h * 128:(h + 1) * 128])

    if parts[1]:
        finish(0)

        def step(t, carry):
            finish(t)
            row_logs(t - 1)
            return carry

        lax.fori_loop(1, 16, step, 0)
        row_logs(15)

    def spread(t):
        for h in range(2):
            v = jnp.broadcast_to(UV[h, pl.ds(t, 1), :], (128, 128))
            FB[t, h * 128:(h + 1) * 128, :] = v.T

    def each_tile(visit):
        spread(0)

        def body(t, carry):
            spread(lax.min(t + 1, 15))
            visit(t)
            return carry

        lax.fori_loop(0, 16, body, 0)

    def block(p, h):
        return S[p, :, h * 128:(h + 1) * 128].reshape(wide)

    def column_logs(t):
        add = FB[t].reshape(wide)
        for s in range(2):
            p = s * 16 + t
            for h in range(2):
                c = block(p, h) + add
                m8 = jnp.max(c, axis=0)
                e = jnp.exp2(c - m8[None])
                S[p, :, h * 128:(h + 1) * 128] = e.reshape(TILE, 128)
                M8[h, p] = m8
                s8 = jnp.sum(e, axis=0)
                top = jnp.max(m8, axis=0, keepdims=True)
                MS[h, pl.ds(p, 1), :] = top
                QS[h, pl.ds(p, 1), :] = jnp.sum(s8 * jnp.exp2(m8 - top), axis=0, keepdims=True)

    def row_sums(it):
        def body(t, carry):
            total = jnp.zeros(wide, jnp.float32)
            for s in range(2):
                p = s * 16 + t
                for h in range(2):
                    total += block(p, h) * W8[h, p][None]
            value = jnp.sum(total.reshape(TILE, 128), axis=1, keepdims=True)
            for h in range(2):
                RC[it, col, h, pl.ds(t, 1), :] = to_row(value[h * 128:(h + 1) * 128])
            return carry

        lax.fori_loop(0, 16, body, 0, unroll=2)

    def column_sums(t):
        by = FB[t].reshape(wide)
        for s in range(2):
            p = s * 16 + t
            for h in range(2):
                s8 = jnp.sum(block(p, h) * by, axis=0) * W8[h, p]
                QS[h, pl.ds(p, 1), :] = jnp.sum(s8, axis=0, keepdims=True)

    def merged(got):
        top = jnp.max(got, axis=0)
        return top + log2(jnp.sum(jnp.exp2(got - top[None]), axis=0))

    def exchange(buf, it, me, n, peer, rsem):
        for k in range(1, n):
            pltpu.make_async_remote_copy(
                src_ref=buf.at[it, me], dst_ref=buf.at[it, me],
                send_sem=es.at[0], recv_sem=rsem.at[it],
                device_id=peer(k), device_id_type=MESH,
            ).start()
        others = buf.at[it, pl.ds(0, n - 1)]
        pltpu.make_async_copy(others, others, rsem.at[it]).wait()

    def mass(ref, h):
        return ref[pl.ds(h, 16, stride=2), :]

    def put(ref, h, v):
        ref[pl.ds(h, 16, stride=2), :] = v

    if parts[3]:
        exchange(RC, 0, col, ncol, col_peer, cr)
    for h in range(2):
        f = log2(mass(sm, h)) - merged(RC[0, :, h])
        FV[h] = f
        UV[h] = f
    if parts[2]:
        each_tile(column_logs)
    for h in range(2):
        one = MS[h] + log2(QS[h])
        for u in range(16):
            named = IV[...] == float(u)
            top = jnp.max(jnp.where(named, one, NEG), axis=0, keepdims=True)
            total = jnp.sum(jnp.where(named, jnp.exp2(one - top), 0.0), axis=0, keepdims=True)
            RR[0, row, h, pl.ds(u, 1), :] = top + log2(jnp.maximum(total, 1e-30))
    if parts[4]:
        exchange(RR, 0, row, nrow, row_peer, rs)
    for h in range(2):
        GV[h] = log2(mass(tm, h)) - merged(RR[0, :, h])

    def weigh(first):
        def body(t, carry):
            for s in range(2):
                p = s * 16 + t
                for h in range(2):
                    if first:
                        g = GV[h, pl.ds(ti[s, t], 1), :]
                        W8[h, p] = jnp.exp2(M8[h, p] + (g if s == 0 else g + idle(t)))
                    else:
                        W8[h, p] = W8[h, p] * UV[h, pl.ds(ti[s, t], 1), :]
            return carry

        lax.fori_loop(0, 16, body, 0, unroll=4)

    for it in range(1, ITERS):
        if parts[2]:
            weigh(it == 1)
            row_sums(it)
        if parts[3]:
            exchange(RC, it, col, ncol, col_peer, cr)
        for h in range(2):
            u = mass(sm, h) / jnp.sum(RC[it, :, h], axis=0)
            UV[h] = u
            if it == ITERS - 1:
                put(f_out, h, (FV[h] + log2(u)) * LN2)
        if parts[2]:
            each_tile(column_sums)
        for h in range(2):
            one = QS[h]
            for u in range(16):
                named = IV[...] == float(u)
                RR[it, row, h, pl.ds(u, 1), :] = jnp.sum(jnp.where(named, one, 0.0), axis=0, keepdims=True)
        if parts[4]:
            exchange(RR, it, row, nrow, row_peer, rs)
        for h in range(2):
            v = mass(tm, h) / jnp.sum(RR[it, :, h], axis=0)
            UV[h] = v
            GV[h] = GV[h] + log2(v)
            if it == ITERS - 1:
                put(g_out, h, GV[h] * LN2)

    if parts[0]:
        for link in range(4):
            quarter = X.at[pl.ds(0, 960)]
            pltpu.make_async_copy(quarter, quarter, gs.at[link]).wait()
    if parts[3] and parts[4]:
        sent = X.at[pl.ds(0, 8 * ITERS * (nrow + ncol - 2))]
        pltpu.make_async_copy(sent, sent, es.at[0]).wait()


def build(mesh, parts):
    ncol = mesh.shape["col"]
    nrow = mesh.shape["row"]
    nx = ny = math.isqrt(nrow)

    def on_device(source_points, target_points, source_mass, target_mass, tile_index, tile_count):
        n, d = source_points.shape
        m = target_points.shape[0]
        vmem = pl.BlockSpec(memory_space=pltpu.VMEM)
        smem = pl.BlockSpec(memory_space=pltpu.SMEM)
        hbm = pl.BlockSpec(memory_space=pl.ANY)
        f32 = jnp.float32
        f, g = pl.pallas_call(
            functools.partial(kernel, nx, ny, ncol, parts),
            out_shape=(
                jax.ShapeDtypeStruct((n // 128, 128), f32),
                jax.ShapeDtypeStruct((m // 128, 128), f32),
            ),
            in_specs=[smem, smem, vmem, vmem, hbm, hbm, vmem, vmem],
            out_specs=(vmem, vmem),
            scratch_shapes=[
                pltpu.VMEM((n, d), jnp.bfloat16),
                *[pltpu.VMEM((256, m), jnp.bfloat16) for _ in range(4)],
                pltpu.VMEM((32, TILE, TILE), f32),
                pltpu.VMEM((2, TILE, 128), f32),
                pltpu.VMEM((16, TILE, 128), f32),
                pltpu.VMEM((2, 32, 128), f32),
                pltpu.VMEM((2, 32, 128), f32),
                pltpu.VMEM((2, 32, 8, 128), f32),
                pltpu.VMEM((2, 32, 8, 128), f32),
                pltpu.VMEM((2, 16, 128), f32),
                pltpu.VMEM((2, 16, 128), f32),
                pltpu.VMEM((2, 16, 128), f32),
                pltpu.VMEM((ITERS, ncol, 2, 16, 128), f32),
                pltpu.VMEM((ITERS, nrow, 2, 16, 128), f32),
                pltpu.VMEM((32, 128), f32),
                pltpu.SemaphoreType.DMA((2,)),
                pltpu.SemaphoreType.DMA((4,)),
                pltpu.SemaphoreType.DMA((30,)),
                pltpu.SemaphoreType.DMA((ITERS,)),
                pltpu.SemaphoreType.DMA((ITERS,)),
                pltpu.SemaphoreType.DMA((1,)),
            ],
            compiler_params=pltpu.CompilerParams(
                collective_id=0, has_side_effects=True, vmem_limit_bytes=60 * 2**20
            ),
        )(
            tile_index.T, tile_count.T, tile_index.T, tile_count.T, source_points, target_points.T,
            source_mass.reshape(-1, 128), target_mass.reshape(-1, 128),
        )
        return f.reshape(-1), g.reshape(-1)

    placed = (P("row", None), P("col", "row"), P("row"), P("col"), P("row", "col"), P("row", "col"))
    return jax.shard_map(
        on_device, mesh=mesh, in_specs=placed, out_specs=(P("row"), P("col")), check_vma=False
    )


def solution(mesh):
    return build(mesh, (True,) * 5)
```

time: 125 us -> 117 us (0.936)
  Pallas kernels: 122 us -> 113 us
  local copies, waits for them, and re-layouts: 0 us -> 2.65 us
  other arithmetic: 1.35 us -> 0 us
    pallas_call x1, Pallas kernels: 122 us -> 113 us  [on_device(): pl.pallas_call(functools.partial(kernel, nx, ny, ncol, parts), out_shape=...]
    unnamed x0 -> x2, local copies, waits for them, and re-layouts: none -> 2.65 us
    reshape x1 -> x0, other arithmetic: 1.35 us -> none  [on_device(): return ((f * LN2).reshape(-1), (g * LN2).reshape(-1))]
where the time goes in v2:
time: 117 us; the launch traced here: 116 us
  Pallas kernels  113 us (97%)
  local copies, waits for them, and re-layouts  2.65 us (2%)
    pallas_call x1, Pallas kernels, on_device(): pl.pallas_call(functools.partial(kernel, nx, ny, ncol, parts), out_shape=...  113 us
    unnamed x2, local copies, waits for them, and re-layouts  2.65 us

profile of v2, /device:TPU:0, one launch (start us, length us, event | category | flops | bytes accessed | tf_op | source)
XLA Modules:
  0.0 116.0 jit_solution(2922963398625929890)
XLA Ops:
  0.6 112.8 %shard_map.77 = (f32[32,128]{1,0:T(8,128)}, f32[32,128]{1,0:T(8,128)}) custom-call(s32[2,16]{1,0:T(2,128)} %bitcast.12, s32[1,16]{1,0:T(1,128)} %bitcast.14, s32[2,16]{1,0:T(2,128)} %bitcast.13, s32[1,16]{1,0:T(1,128)} %bitcast.15, bf16[4096,1024]{1,0:T(8,128)(2,1)} %sp.1, bf16[64,4096]{1,0:T(8,128)(2,1)} %bitcast.7, f32[32,128]{1,0:T(8,128)} %bitcast.8, ...), custom_call_target="tpu_custom_call" | custom-call | tf_op jit(solution)/shard_map/pallas_call | solution.py:374
  113.4 1.3 %copy.10 = f32[4096]{0:T(1024)} copy(f32[4096]{0:T(1024)} %bitcast.11) | data formatting | bytes 32768
  114.7 1.3 %copy.11 = f32[4096]{0:T(1024)} copy(f32[4096]{0:T(1024)} %bitcast.10) | data formatting | bytes 32768

commit v3 on v2

--- a/solution.py
+++ b/solution.py
@@ -25,7 +25,7 @@
 def kernel(
     nx, ny, ncol, parts,
     ti, tc, tv, cv, sp, tp, sm, tm, f_out, g_out,
-    X, T0, T1, T2, T3, S, MB, FB, MS, QS, M8, W8, FV, GV, UV, RC, RR, IV,
+    X, T0, T1, T2, T3, S, SP, KA, KB, TB, MA, MC, MS, QS, M8, W8, FV, GV, UV, RC, RR, IV,
     lsem, gs, gr, cr, rs, es,
 ):
     T = (T0, T1, T2, T3)
@@ -112,23 +112,29 @@
 
     scale = LOG2E / math.sqrt(sp.shape[1])
     wide = (32, 8, 128)
-    diagonal = lax.broadcasted_iota(jnp.int32, (128, 128), 0) == lax.broadcasted_iota(jnp.int32, (128, 128), 1)
-
-    def to_row(v):
-        return jnp.sum(jnp.where(diagonal, jnp.broadcast_to(v, (128, 128)), 0.0), axis=0, keepdims=True)
-
-    def product(d, t, s):
-        cols = pl.ds(pl.multiple_of(lax.rem(x + d, nx) * 256, 256), 256)
-        left = X[pl.ds(pl.multiple_of(t * TILE, TILE), TILE), cols]
-        right = T[d][:, pl.ds(ti[s, t] * TILE, TILE)]
-        return jnp.dot(left, right, preferred_element_type=jnp.float32) * scale
-
-    def scores(d):
+
+    def fold(op, v):
+        v = v.reshape((v.shape[0] // 4, 4) + v.shape[1:])
+        v = functools.reduce(op, [v[k] for k in range(v.shape[0])])
+        while v.shape[0] > 1:
+            n = v.shape[0] // 2
+            v = op(v[:n], v[n:])
+        return v[0]
+
+    def product(chunks, t, s):
+        here = pl.ds(pl.multiple_of(t * TILE, TILE), TILE)
+        left = [X[here, pl.ds(pl.multiple_of(lax.rem(x + d, nx) * 256, 256), 256)] for d in chunks]
+        right = [T[d][:, pl.ds(ti[s, t] * TILE, TILE)] for d in chunks]
+        return jnp.dot(
+            jnp.concatenate(left, axis=1), jnp.concatenate(right, axis=0), preferred_element_type=jnp.float32
+        ) * scale
+
+    def scores(*chunks):
         def body(t, carry):
             for s in range(2):
                 p = s * 16 + t
-                new = product(d, t, s)
-                S[p] = new if d == 0 else S[p] + new
+                new = product(chunks, t, s)
+                SP[p] = new if chunks == (0,) else SP[p] + new
             return carry
 
         lax.fori_loop(0, 16, body, 0)
@@ -177,96 +183,129 @@
         fbx2 = forward_x(bx2, 2, B0, B1)
         done(fay3, fay1)
     if parts[1]:
-        scores(3)
-        scores(1)
+        scores(3, 1)
     if parts[0]:
         done(fbx0, fbx3, fbx1, fay2, fbx2)
 
-    def finish(t):
+    def over_lanes(op, v):
+        v = fold(op, v.T.reshape(16, 8, 128))
+        n = 8
+        while n > 1:
+            n //= 2
+            v = op(v[:n], v[n:])
+        return v
+
+    def as_column(v):
+        return jnp.broadcast_to(v, (128, 128)).T
+
+    def finish(t, K):
         tops = []
         for s in range(2):
             p = s * 16 + t
-            r = S[p] + product(2, t, s)
-            S[p] = r
+            r = SP[p] + product((2,), t, s)
+            if s:
+                r = r + idle(t)
+            for h in range(2):
+                S[h, p] = r[:, h * 128:(h + 1) * 128]
+                K[s, h] = r[:, h * 128:(h + 1) * 128]
             tops.append(jnp.maximum(r[:, :128], r[:, 128:]))
-        top = jnp.max(jnp.maximum(tops[0], tops[1] + idle(t)), axis=1, keepdims=True)
-        MB[lax.rem(t, 2)] = jnp.broadcast_to(top, (TILE, 128))
-
-    def row_logs(t):
-        top = MB[lax.rem(t, 2)]
-        total = jnp.zeros((TILE, 128), jnp.float32)
-        for s in range(2):
-            shift = top if s == 0 else top - idle(t)
-            for h in range(2):
-                total += jnp.exp2(S[s * 16 + t, :, h * 128:(h + 1) * 128] - shift)
-        value = top[:, :1] + log2(jnp.sum(total, axis=1, keepdims=True))
-        for h in range(2):
-            RC[0, col, h, pl.ds(t, 1), :] = to_row(value[h * 128:(h + 1) * 128])
+        TB[...] = jnp.maximum(tops[0], tops[1])
+
+    def row_tops(t):
+        for h in range(2):
+            part = slice(h * 128, (h + 1) * 128)
+            line = over_lanes(jnp.maximum, TB[part, :])
+            MS[h, pl.ds(t, 1), :] = line
+            MA[part, :] = as_column(line)
+
+    def row_exps(K):
+        top = MA[...]
+        e = [jnp.exp2(K[s, k] - top) for s in range(2) for k in range(2)]
+        MC[...] = (e[0] + e[1]) + (e[2] + e[3])
+
+    def row_totals(t):
+        for h in range(2):
+            QS[h, pl.ds(t, 1), :] = over_lanes(jnp.add, MC[h * 128:(h + 1) * 128, :])
 
     if parts[1]:
-        finish(0)
-
-        def step(t, carry):
-            finish(t)
-            row_logs(t - 1)
+        def stages(t, K, now):
+            if 3 in now:
+                row_totals(t - 3)
+            if 2 in now:
+                row_exps(K)
+            if 1 in now:
+                row_tops(t - 1)
+            if 0 in now:
+                finish(t, K)
+
+        def step(k, carry):
+            stages(2 * k, KA, (3, 2, 1, 0))
+            stages(2 * k + 1, KB, (3, 2, 1, 0))
             return carry
 
-        lax.fori_loop(1, 16, step, 0)
-        row_logs(15)
-
-    def spread(t):
-        for h in range(2):
-            v = jnp.broadcast_to(UV[h, pl.ds(t, 1), :], (128, 128))
-            FB[t, h * 128:(h + 1) * 128, :] = v.T
+        stages(0, KA, (0,))
+        stages(1, KB, (1, 0))
+        stages(2, KA, (2, 1, 0))
+        stages(3, KB, (3, 2, 1, 0))
+        lax.fori_loop(2, 8, step, 0)
+        stages(16, KA, (3, 2, 1))
+        stages(17, KB, (3, 2))
+        stages(18, KA, (3,))
+    for h in range(2):
+        RC[0, col, h] = MS[h, :16] + log2(QS[h, :16])
+
+    def spread(t, to):
+        for h in range(2):
+            to[h * 128:(h + 1) * 128, :] = as_column(UV[h, pl.ds(t, 1), :])
 
     def each_tile(visit):
-        spread(0)
-
-        def body(t, carry):
-            spread(lax.min(t + 1, 15))
-            visit(t)
+        spread(0, MA)
+
+        def body(k, carry):
+            t = 2 * k
+            spread(t + 1, MC)
+            visit(t, MA)
+            spread(lax.min(t + 2, 15), MA)
+            visit(t + 1, MC)
             return carry
 
-        lax.fori_loop(0, 16, body, 0)
+        lax.fori_loop(0, 8, body, 0)
 
     def block(p, h):
-        return S[p, :, h * 128:(h + 1) * 128].reshape(wide)
-
-    def column_logs(t):
-        add = FB[t].reshape(wide)
+        return S[h, p].reshape(wide)
+
+    def column_logs(t, by):
+        add = by[...].reshape(wide)
         for s in range(2):
             p = s * 16 + t
             for h in range(2):
                 c = block(p, h) + add
-                m8 = jnp.max(c, axis=0)
+                m8 = fold(jnp.maximum, c)
                 e = jnp.exp2(c - m8[None])
-                S[p, :, h * 128:(h + 1) * 128] = e.reshape(TILE, 128)
+                S[h, p] = e.reshape(TILE, 128)
                 M8[h, p] = m8
-                s8 = jnp.sum(e, axis=0)
+                s8 = fold(jnp.add, e)
                 top = jnp.max(m8, axis=0, keepdims=True)
                 MS[h, pl.ds(p, 1), :] = top
                 QS[h, pl.ds(p, 1), :] = jnp.sum(s8 * jnp.exp2(m8 - top), axis=0, keepdims=True)
 
     def row_sums(it):
         def body(t, carry):
-            total = jnp.zeros(wide, jnp.float32)
-            for s in range(2):
-                p = s * 16 + t
-                for h in range(2):
-                    total += block(p, h) * W8[h, p][None]
-            value = jnp.sum(total.reshape(TILE, 128), axis=1, keepdims=True)
+            e = [block(s * 16 + t, h) * W8[h, s * 16 + t][None] for s in range(2) for h in range(2)]
+            total = (e[0] + e[1]) + (e[2] + e[3])
+            total = total.reshape(TILE, 128)
             for h in range(2):
-                RC[it, col, h, pl.ds(t, 1), :] = to_row(value[h * 128:(h + 1) * 128])
+                RC[it, col, h, pl.ds(t, 1), :] = over_lanes(jnp.add, total[h * 128:(h + 1) * 128])
             return carry
 
         lax.fori_loop(0, 16, body, 0, unroll=2)
 
-    def column_sums(t):
-        by = FB[t].reshape(wide)
+    def column_sums(t, by):
+        by = by[...].reshape(wide)
         for s in range(2):
             p = s * 16 + t
             for h in range(2):
-                s8 = jnp.sum(block(p, h) * by, axis=0) * W8[h, p]
+                s8 = fold(jnp.add, block(p, h) * by) * W8[h, p]
                 QS[h, pl.ds(p, 1), :] = jnp.sum(s8, axis=0, keepdims=True)
 
     def merged(got):
@@ -333,7 +372,7 @@
             u = mass(sm, h) / jnp.sum(RC[it, :, h], axis=0)
             UV[h] = u
             if it == ITERS - 1:
-                put(f_out, h, (FV[h] + log2(u)) * LN2)
+                put(f_out, h, FV[h] + log2(u))
         if parts[2]:
             each_tile(column_sums)
         for h in range(2):
@@ -348,7 +387,7 @@
             UV[h] = v
             GV[h] = GV[h] + log2(v)
             if it == ITERS - 1:
-                put(g_out, h, GV[h] * LN2)
+                put(g_out, h, GV[h])
 
     if parts[0]:
         for link in range(4):
@@ -382,9 +421,13 @@
             scratch_shapes=[
                 pltpu.VMEM((n, d), jnp.bfloat16),
                 *[pltpu.VMEM((256, m), jnp.bfloat16) for _ in range(4)],
+                pltpu.VMEM((2, 32, TILE, 128), f32),
                 pltpu.VMEM((32, TILE, TILE), f32),
-                pltpu.VMEM((2, TILE, 128), f32),
-                pltpu.VMEM((16, TILE, 128), f32),
+                pltpu.VMEM((2, 2, TILE, 128), f32),
+                pltpu.VMEM((2, 2, TILE, 128), f32),
+                pltpu.VMEM((TILE, 128), f32),
+                pltpu.VMEM((TILE, 128), f32),
+                pltpu.VMEM((TILE, 128), f32),
                 pltpu.VMEM((2, 32, 128), f32),
                 pltpu.VMEM((2, 32, 128), f32),
                 pltpu.VMEM((2, 32, 8, 128), f32),
@@ -409,7 +452,7 @@
             tile_index.T, tile_count.T, tile_index.T, tile_count.T, source_points, target_points.T,
             source_mass.reshape(-1, 128), target_mass.reshape(-1, 128),
         )
-        return f.reshape(-1), g.reshape(-1)
+        return (f * LN2).reshape(-1), (g * LN2).reshape(-1)
 
     placed = (P("row", None), P("col", "row"), P("row"), P("col"), P("row", "col"), P("row", "col"))
     return jax.shard_map(

time: 117 us -> 103 us (0.88)
  Pallas kernels: 113 us -> 101 us
  local copies, waits for them, and re-layouts: 2.65 us -> 0 us
  other arithmetic: 0 us -> 1.35 us
    pallas_call x1, Pallas kernels: 113 us -> 101 us  [on_device(): pl.pallas_call(functools.partial(kernel, nx, ny, ncol, parts), out_shape=...]
    unnamed x2 -> x0, local copies, waits for them, and re-layouts: 2.65 us -> none
    reshape x0 -> x1, other arithmetic: none -> 1.35 us  [on_device(): return ((f * LN2).reshape(-1), (g * LN2).reshape(-1))]
where the time goes in v3:
time: 103 us
  Pallas kernels  101 us (98%)
  other arithmetic  1.35 us (1%)
    pallas_call x1, Pallas kernels, on_device(): pl.pallas_call(functools.partial(kernel, nx, ny, ncol, parts), out_shape=...  101 us

profile of v3, /device:TPU:0, one launch (start us, length us, event | category | flops | bytes accessed | tf_op | source)
XLA Modules:
  0.0 102.6 jit_solution(5864526575918676670)
XLA Ops:
  0.6 100.6 %shard_map.77 = (f32[32,128]{1,0:T(8,128)}, f32[32,128]{1,0:T(8,128)}) custom-call(s32[2,16]{1,0:T(2,128)} %bitcast.12, s32[1,16]{1,0:T(1,128)} %bitcast.14, s32[2,16]{1,0:T(2,128)} %bitcast.13, s32[1,16]{1,0:T(1,128)} %bitcast.15, bf16[4096,1024]{1,0:T(8,128)(2,1)} %sp.1, bf16[64,4096]{1,0:T(8,128)(2,1)} %bitcast.9, f32[32,128]{1,0:T(8,128)} %bitcast.10, ...), custom_call_target="tpu_custom_call" | custom-call | tf_op jit(solution)/shard_map/pallas_call | solution.py:413
  101.2 1.4 %multiply_bitcast_fusion = (f32[4096]{0:T(1024)}, f32[4096]{0:T(1024)}) fusion(f32[32,128]{1,0:T(8,128)} %get-tuple-element.5, f32[32,128]{1,0:T(8,128)} %get-tuple-element.4), kind=kLoop, calls=%fused_computation | loop fusion | flops 8192 | bytes 65536 | tf_op jit(solution)/shard_map/reshape | solution.py:455

commit v4 on v3

--- a/solution.py
+++ b/solution.py
@@ -24,8 +24,8 @@
 
 def kernel(
     nx, ny, ncol, parts,
-    ti, tc, tv, cv, sp, tp, sm, tm, f_out, g_out,
-    X, T0, T1, T2, T3, S, SP, KA, KB, TB, MA, MC, MS, QS, M8, W8, FV, GV, UV, RC, RR, IV,
+    ti_hbm, tc_hbm, sp, tp, sm_hbm, tm_hbm, f_out, g_out,
+    ti, tc, tv, cv, sm, tm, X, T0, T1, T2, T3, S, SP, MA, MC, RT, MS, QS, M8, W8, FV, GV, UV, RC, RR, IV,
     lsem, gs, gr, cr, rs, es,
 ):
     T = (T0, T1, T2, T3)
@@ -43,6 +43,14 @@
     def col_peer(k):
         return (row, lax.rem(col + k, ncol))
 
+    tables = [
+        pltpu.make_async_copy(a, b, lsem.at[2 + k])
+        for k, (a, b) in enumerate(
+            ((ti_hbm, ti), (tc_hbm, tc), (ti_hbm, tv), (tc_hbm, cv), (sm_hbm, sm), (tm_hbm, tm))
+        )
+    ]
+    for c in tables:
+        c.start()
     load_x = pltpu.make_async_copy(sp, X, lsem.at[0])
     load_x.start()
 
@@ -150,6 +158,8 @@
     keep = pltpu.make_async_copy(tp, T[0].at[rows(0), :], lsem.at[1])
     keep.start()
 
+    for c in tables:
+        c.wait()
     small = lax.broadcasted_iota(jnp.int32, (16, 16), 0) == lax.broadcasted_iota(jnp.int32, (16, 16), 1)
     for s in range(2):
         name = jnp.where(cv[...] > s, tv[s:s + 1, :], -1).astype(jnp.float32)
@@ -187,6 +197,40 @@
     if parts[0]:
         done(fbx0, fbx3, fbx1, fay2, fbx2)
 
+    def give(buf, it, part, me, n, peer, rsem):
+        for k in range(1, n):
+            pltpu.make_async_remote_copy(
+                src_ref=buf.at[it, part, me], dst_ref=buf.at[it, part, me],
+                send_sem=es.at[0], recv_sem=rsem.at[it, part],
+                device_id=peer(k), device_id_type=MESH,
+            ).start()
+
+    def take(buf, it, part, n, rsem):
+        others = buf.at[it, part, pl.ds(0, n - 1)]
+        pltpu.make_async_copy(others, others, rsem.at[it, part]).wait()
+
+    def give_rows(it, half):
+        if parts[3]:
+            give(RC, it, half, col, ncol, col_peer, cr)
+
+    def take_rows(it, half):
+        if parts[3]:
+            take(RC, it, half, ncol, cr)
+
+    def give_columns(it, h):
+        if parts[4]:
+            give(RR, it, h, row, nrow, row_peer, rs)
+
+    def take_columns(it, h):
+        if parts[4]:
+            take(RR, it, h, nrow, rs)
+
+    def log_rows(half):
+        eight = slice(half * 8, half * 8 + 8)
+        for h in range(2):
+            RC[0, half, col, h] = MS[h, eight] + log2(QS[h, eight])
+        give_rows(0, half)
+
     def over_lanes(op, v):
         v = fold(op, v.T.reshape(16, 8, 128))
         n = 8
@@ -198,87 +242,83 @@
     def as_column(v):
         return jnp.broadcast_to(v, (128, 128)).T
 
-    def finish(t, K):
-        tops = []
+    def finish(t, to):
+        r = []
         for s in range(2):
             p = s * 16 + t
-            r = SP[p] + product((2,), t, s)
+            both = SP[p] + product((2,), t, s)
             if s:
-                r = r + idle(t)
+                both = both + idle(t)
             for h in range(2):
-                S[h, p] = r[:, h * 128:(h + 1) * 128]
-                K[s, h] = r[:, h * 128:(h + 1) * 128]
-            tops.append(jnp.maximum(r[:, :128], r[:, 128:]))
-        TB[...] = jnp.maximum(tops[0], tops[1])
-
-    def row_tops(t):
+                S[h, p] = both[:, h * 128:(h + 1) * 128]
+                r.append(both[:, h * 128:(h + 1) * 128])
+        top = jnp.maximum(jnp.maximum(r[0], r[1]), jnp.maximum(r[2], r[3]))
+        e = [jnp.exp2(v - top) for v in r]
+        to[...] = top + log2((e[0] + e[1]) + (e[2] + e[3]))
+
+    def row_logs(t, logs):
         for h in range(2):
-            part = slice(h * 128, (h + 1) * 128)
-            line = over_lanes(jnp.maximum, TB[part, :])
-            MS[h, pl.ds(t, 1), :] = line
-            MA[part, :] = as_column(line)
-
-    def row_exps(K):
-        top = MA[...]
-        e = [jnp.exp2(K[s, k] - top) for s in range(2) for k in range(2)]
-        MC[...] = (e[0] + e[1]) + (e[2] + e[3])
-
-    def row_totals(t):
-        for h in range(2):
-            QS[h, pl.ds(t, 1), :] = over_lanes(jnp.add, MC[h * 128:(h + 1) * 128, :])
+            v = logs[h * 128:(h + 1) * 128, :].T.reshape(16, 8, 128)
+            m8 = fold(jnp.maximum, v)
+            s8 = fold(jnp.add, jnp.exp2(v - m8[None]))
+            top = jnp.max(m8, axis=0, keepdims=True)
+            MS[h, pl.ds(t, 1), :] = top
+            QS[h, pl.ds(t, 1), :] = jnp.sum(s8 * jnp.exp2(m8 - top), axis=0, keepdims=True)
 
     if parts[1]:
-        def stages(t, K, now):
-            if 3 in now:
-                row_totals(t - 3)
-            if 2 in now:
-                row_exps(K)
-            if 1 in now:
-                row_tops(t - 1)
-            if 0 in now:
-                finish(t, K)
-
         def step(k, carry):
-            stages(2 * k, KA, (3, 2, 1, 0))
-            stages(2 * k + 1, KB, (3, 2, 1, 0))
-            return carry
-
-        stages(0, KA, (0,))
-        stages(1, KB, (1, 0))
-        stages(2, KA, (2, 1, 0))
-        stages(3, KB, (3, 2, 1, 0))
-        lax.fori_loop(2, 8, step, 0)
-        stages(16, KA, (3, 2, 1))
-        stages(17, KB, (3, 2))
-        stages(18, KA, (3,))
-    for h in range(2):
-        RC[0, col, h] = MS[h, :16] + log2(QS[h, :16])
+            finish(2 * k + 1, MC)
+            row_logs(2 * k, MA)
+            finish(2 * k + 2, MA)
+            row_logs(2 * k + 1, MC)
+            return carry
+
+        finish(0, MA)
+        lax.fori_loop(0, 4, step, 0)
+    log_rows(0)
+    if parts[1]:
+        lax.fori_loop(4, 7, step, 0)
+        finish(15, MC)
+        row_logs(14, MA)
+        row_logs(15, MC)
+    log_rows(1)
 
     def spread(t, to):
         for h in range(2):
             to[h * 128:(h + 1) * 128, :] = as_column(UV[h, pl.ds(t, 1), :])
 
-    def each_tile(visit):
-        spread(0, MA)
+    def each_tile(visit, half, keep):
+        spread(8 * half, MA)
 
         def body(k, carry):
-            t = 2 * k
+            t = 8 * half + 2 * k
             spread(t + 1, MC)
             visit(t, MA)
+            if keep:
+                RT[t] = MA[...]
             spread(lax.min(t + 2, 15), MA)
             visit(t + 1, MC)
-            return carry
-
-        lax.fori_loop(0, 8, body, 0)
+            if keep:
+                RT[t + 1] = MC[...]
+            return carry
+
+        lax.fori_loop(0, 4, body, 0)
+
+    def each_kept(visit):
+        def body(k, carry):
+            visit(8 + k, RT.at[8 + k])
+            return carry
+
+        lax.fori_loop(0, 8, body, 0, unroll=2)
 
     def block(p, h):
         return S[h, p].reshape(wide)
 
-    def column_logs(t, by):
+    def column_logs(t, by, lanes):
         add = by[...].reshape(wide)
         for s in range(2):
             p = s * 16 + t
-            for h in range(2):
+            for h in lanes:
                 c = block(p, h) + add
                 m8 = fold(jnp.maximum, c)
                 e = jnp.exp2(c - m8[None])
@@ -289,22 +329,31 @@
                 MS[h, pl.ds(p, 1), :] = top
                 QS[h, pl.ds(p, 1), :] = jnp.sum(s8 * jnp.exp2(m8 - top), axis=0, keepdims=True)
 
-    def row_sums(it):
-        def body(t, carry):
-            e = [block(s * 16 + t, h) * W8[h, s * 16 + t][None] for s in range(2) for h in range(2)]
-            total = (e[0] + e[1]) + (e[2] + e[3])
-            total = total.reshape(TILE, 128)
+    def row_parts():
+        def step(t, carry):
+            e = [block(s * 16 + t, 0) * W8[0, s * 16 + t][None] for s in range(2)]
+            RT[t] = (e[0] + e[1]).reshape(TILE, 128)
+            return carry
+
+        lax.fori_loop(0, 16, step, 0, unroll=2)
+
+    def row_sums(it, half):
+        def step(k, carry):
+            t = 8 * half + k
+            e = [block(s * 16 + t, 1) * W8[1, s * 16 + t][None] for s in range(2)]
+            total = RT[t] + (e[0] + e[1]).reshape(TILE, 128)
             for h in range(2):
-                RC[it, col, h, pl.ds(t, 1), :] = over_lanes(jnp.add, total[h * 128:(h + 1) * 128])
-            return carry
-
-        lax.fori_loop(0, 16, body, 0, unroll=2)
-
-    def column_sums(t, by):
+                RC[it, half, col, h, pl.ds(k, 1), :] = over_lanes(jnp.add, total[h * 128:(h + 1) * 128])
+            return carry
+
+        lax.fori_loop(0, 8, step, 0, unroll=2)
+        give_rows(it, half)
+
+    def column_sums(t, by, lanes):
         by = by[...].reshape(wide)
         for s in range(2):
             p = s * 16 + t
-            for h in range(2):
+            for h in lanes:
                 s8 = fold(jnp.add, block(p, h) * by) * W8[h, p]
                 QS[h, pl.ds(p, 1), :] = jnp.sum(s8, axis=0, keepdims=True)
 
@@ -312,82 +361,98 @@
         top = jnp.max(got, axis=0)
         return top + log2(jnp.sum(jnp.exp2(got - top[None]), axis=0))
 
-    def exchange(buf, it, me, n, peer, rsem):
-        for k in range(1, n):
-            pltpu.make_async_remote_copy(
-                src_ref=buf.at[it, me], dst_ref=buf.at[it, me],
-                send_sem=es.at[0], recv_sem=rsem.at[it],
-                device_id=peer(k), device_id_type=MESH,
-            ).start()
-        others = buf.at[it, pl.ds(0, n - 1)]
-        pltpu.make_async_copy(others, others, rsem.at[it]).wait()
-
-    def mass(ref, h):
+    def mass(ref, h, half):
+        return ref[pl.ds(16 * half + h, 8, stride=2), :]
+
+    def all_mass(ref, h):
         return ref[pl.ds(h, 16, stride=2), :]
 
-    def put(ref, h, v):
-        ref[pl.ds(h, 16, stride=2), :] = v
-
-    if parts[3]:
-        exchange(RC, 0, col, ncol, col_peer, cr)
-    for h in range(2):
-        f = log2(mass(sm, h)) - merged(RC[0, :, h])
-        FV[h] = f
-        UV[h] = f
-    if parts[2]:
-        each_tile(column_logs)
-    for h in range(2):
+    def columns(it, visit, combine, ready):
+        ready(0)
+        if parts[2]:
+            each_tile(functools.partial(visit, lanes=(0, 1)), 0, False)
+        ready(1)
+        for h in range(2):
+            if parts[2] and h == 0:
+                each_tile(functools.partial(visit, lanes=(h,)), 1, True)
+            elif parts[2]:
+                each_kept(functools.partial(visit, lanes=(h,)))
+            combine(h)
+            give_columns(it, h)
+
+    def first_rows(half):
+        take_rows(0, half)
+        eight = slice(half * 8, half * 8 + 8)
+        for h in range(2):
+            f = log2(mass(sm, h, half)) - merged(RC[0, half, :, h])
+            FV[h, eight] = f
+            UV[h, eight] = f
+
+    def first_columns(h):
         one = MS[h] + log2(QS[h])
         for u in range(16):
             named = IV[...] == float(u)
             top = jnp.max(jnp.where(named, one, NEG), axis=0, keepdims=True)
             total = jnp.sum(jnp.where(named, jnp.exp2(one - top), 0.0), axis=0, keepdims=True)
-            RR[0, row, h, pl.ds(u, 1), :] = top + log2(jnp.maximum(total, 1e-30))
-    if parts[4]:
-        exchange(RR, 0, row, nrow, row_peer, rs)
-    for h in range(2):
-        GV[h] = log2(mass(tm, h)) - merged(RR[0, :, h])
-
-    def weigh(first):
+            RR[0, h, row, pl.ds(u, 1), :] = top + log2(jnp.maximum(total, 1e-30))
+
+    columns(0, column_logs, first_columns, first_rows)
+
+    def weigh(first, h):
         def body(t, carry):
             for s in range(2):
                 p = s * 16 + t
-                for h in range(2):
-                    if first:
-                        g = GV[h, pl.ds(ti[s, t], 1), :]
-                        W8[h, p] = jnp.exp2(M8[h, p] + (g if s == 0 else g + idle(t)))
-                    else:
-                        W8[h, p] = W8[h, p] * UV[h, pl.ds(ti[s, t], 1), :]
-            return carry
-
-        lax.fori_loop(0, 16, body, 0, unroll=4)
+                if first:
+                    g = GV[h, pl.ds(ti[s, t], 1), :]
+                    W8[h, p] = jnp.exp2(M8[h, p] + (g if s == 0 else g + idle(t)))
+                else:
+                    W8[h, p] = W8[h, p] * UV[h, pl.ds(ti[s, t], 1), :]
+            return carry
+
+        lax.fori_loop(0, 16, body, 0, unroll=8)
+
+    def columns_arrive(it, h):
+        take_columns(it, h)
+        if it == 0:
+            GV[h] = log2(all_mass(tm, h)) - merged(RR[0, h])
+        else:
+            v = all_mass(tm, h) / jnp.sum(RR[it, h], axis=0)
+            UV[h] = v
+            GV[h] = GV[h] + log2(v)
 
     for it in range(1, ITERS):
-        if parts[2]:
-            weigh(it == 1)
-            row_sums(it)
-        if parts[3]:
-            exchange(RC, it, col, ncol, col_peer, cr)
         for h in range(2):
-            u = mass(sm, h) / jnp.sum(RC[it, :, h], axis=0)
-            UV[h] = u
-            if it == ITERS - 1:
-                put(f_out, h, FV[h] + log2(u))
-        if parts[2]:
-            each_tile(column_sums)
-        for h in range(2):
+            columns_arrive(it - 1, h)
+            if parts[2]:
+                weigh(it == 1, h)
+                if h == 0:
+                    row_parts()
+        for half in range(2):
+            if parts[2]:
+                row_sums(it, half)
+            else:
+                give_rows(it, half)
+
+        def rows_arrive(half, it=it):
+            take_rows(it, half)
+            eight = slice(half * 8, half * 8 + 8)
+            for h in range(2):
+                u = mass(sm, h, half) / jnp.sum(RC[it, half, :, h], axis=0)
+                UV[h, eight] = u
+                if it == ITERS - 1:
+                    f_out[pl.ds(16 * half + h, 8, stride=2), :] = FV[h, eight] + log2(u)
+
+        def sum_columns(h, it=it):
             one = QS[h]
             for u in range(16):
                 named = IV[...] == float(u)
-                RR[it, row, h, pl.ds(u, 1), :] = jnp.sum(jnp.where(named, one, 0.0), axis=0, keepdims=True)
-        if parts[4]:
-            exchange(RR, it, row, nrow, row_peer, rs)
-        for h in range(2):
-            v = mass(tm, h) / jnp.sum(RR[it, :, h], axis=0)
-            UV[h] = v
-            GV[h] = GV[h] + log2(v)
-            if it == ITERS - 1:
-                put(g_out, h, GV[h])
+                RR[it, h, row, pl.ds(u, 1), :] = jnp.sum(jnp.where(named, one, 0.0), axis=0, keepdims=True)
+
+        columns(it, column_sums, sum_columns, rows_arrive)
+
+    for h in range(2):
+        columns_arrive(ITERS - 1, h)
+        g_out[pl.ds(h, 16, stride=2), :] = GV[h]
 
     if parts[0]:
         for link in range(4):
@@ -407,7 +472,6 @@
         n, d = source_points.shape
         m = target_points.shape[0]
         vmem = pl.BlockSpec(memory_space=pltpu.VMEM)
-        smem = pl.BlockSpec(memory_space=pltpu.SMEM)
         hbm = pl.BlockSpec(memory_space=pl.ANY)
         f32 = jnp.float32
         f, g = pl.pallas_call(
@@ -416,18 +480,22 @@
                 jax.ShapeDtypeStruct((n // 128, 128), f32),
                 jax.ShapeDtypeStruct((m // 128, 128), f32),
             ),
-            in_specs=[smem, smem, vmem, vmem, hbm, hbm, vmem, vmem],
+            in_specs=[hbm] * 6,
             out_specs=(vmem, vmem),
             scratch_shapes=[
+                pltpu.SMEM(tile_index.shape[::-1], jnp.int32),
+                pltpu.SMEM(tile_count.shape[::-1], jnp.int32),
+                pltpu.VMEM(tile_index.shape[::-1], jnp.int32),
+                pltpu.VMEM(tile_count.shape[::-1], jnp.int32),
+                pltpu.VMEM((n // 128, 128), f32),
+                pltpu.VMEM((m // 128, 128), f32),
                 pltpu.VMEM((n, d), jnp.bfloat16),
                 *[pltpu.VMEM((256, m), jnp.bfloat16) for _ in range(4)],
                 pltpu.VMEM((2, 32, TILE, 128), f32),
                 pltpu.VMEM((32, TILE, TILE), f32),
-                pltpu.VMEM((2, 2, TILE, 128), f32),
-                pltpu.VMEM((2, 2, TILE, 128), f32),
                 pltpu.VMEM((TILE, 128), f32),
                 pltpu.VMEM((TILE, 128), f32),
-                pltpu.VMEM((TILE, 128), f32),
+                pltpu.VMEM((16, TILE, 128), f32),
                 pltpu.VMEM((2, 32, 128), f32),
                 pltpu.VMEM((2, 32, 128), f32),
                 pltpu.VMEM((2, 32, 8, 128), f32),
@@ -435,21 +503,21 @@
                 pltpu.VMEM((2, 16, 128), f32),
                 pltpu.VMEM((2, 16, 128), f32),
                 pltpu.VMEM((2, 16, 128), f32),
-                pltpu.VMEM((ITERS, ncol, 2, 16, 128), f32),
-                pltpu.VMEM((ITERS, nrow, 2, 16, 128), f32),
+                pltpu.VMEM((ITERS, 2, ncol, 2, 8, 128), f32),
+                pltpu.VMEM((ITERS, 2, nrow, 16, 128), f32),
                 pltpu.VMEM((32, 128), f32),
-                pltpu.SemaphoreType.DMA((2,)),
+                pltpu.SemaphoreType.DMA((8,)),
                 pltpu.SemaphoreType.DMA((4,)),
                 pltpu.SemaphoreType.DMA((30,)),
-                pltpu.SemaphoreType.DMA((ITERS,)),
-                pltpu.SemaphoreType.DMA((ITERS,)),
+                pltpu.SemaphoreType.DMA((ITERS, 2)),
+                pltpu.SemaphoreType.DMA((ITERS, 2)),
                 pltpu.SemaphoreType.DMA((1,)),
             ],
             compiler_params=pltpu.CompilerParams(
                 collective_id=0, has_side_effects=True, vmem_limit_bytes=60 * 2**20
             ),
         )(
-            tile_index.T, tile_count.T, tile_index.T, tile_count.T, source_points, target_points.T,
+            tile_index.T, tile_count.T, source_points, target_points.T,
             source_mass.reshape(-1, 128), target_mass.reshape(-1, 128),
         )
         return (f * LN2).reshape(-1), (g * LN2).reshape(-1)

time: 103 us -> 98.9 us (0.960)
  Pallas kernels: 101 us -> 96.7 us
    pallas_call x1, Pallas kernels: 101 us -> 96.7 us  [on_device(): pl.pallas_call(functools.partial(kernel, nx, ny, ncol, parts), out_shape=...]
where the time goes in v4:
time: 98.9 us; the launch traced here: 98.7 us
  Pallas kernels  96.7 us (98%)
  other arithmetic  1.35 us (1%)
    pallas_call x1, Pallas kernels, on_device(): pl.pallas_call(functools.partial(kernel, nx, ny, ncol, parts), out_shape=...  96.7 us

profile of v4, /device:TPU:0, one launch (start us, length us, event | category | flops | bytes accessed | tf_op | source)
XLA Modules:
  0.0 98.7 jit_solution(16072605440736591346)
XLA Ops:
  0.6 96.7 %shard_map.77 = (f32[32,128]{1,0:T(8,128)}, f32[32,128]{1,0:T(8,128)}) custom-call(s32[2,16]{1,0:T(2,128)} %bitcast.12, s32[1,16]{1,0:T(1,128)} %bitcast.13, bf16[4096,1024]{1,0:T(8,128)(2,1)} %sp.1, bf16[64,4096]{1,0:T(8,128)(2,1)} %bitcast.9, f32[32,128]{1,0:T(8,128)} %bitcast.10, f32[32,128]{1,0:T(8,128)} %bitcast.11), custom_call_target="tpu_custom_call" | custom-call | tf_op jit(solution)/shard_map/pallas_call | solution.py:477
  97.4 1.4 %multiply_bitcast_fusion = (f32[4096]{0:T(1024)}, f32[4096]{0:T(1024)}) fusion(f32[32,128]{1,0:T(8,128)} %get-tuple-element.5, f32[32,128]{1,0:T(8,128)} %get-tuple-element.4), kind=kLoop, calls=%fused_computation | loop fusion | flops 8192 | bytes 65536 | tf_op jit(solution)/shard_map/reshape | solution.py:523

commit v5 on v4

--- a/solution.py
+++ b/solution.py
@@ -14,8 +14,9 @@
 LN2 = 0.6931471805599453
 NEG = -1e30
 MESH = pl.DeviceIdType.MESH
-HALF = 2048
-QUART = 1024
+HALF = 16
+QUART = 8
+SHORT = True
 
 
 def log2(v):
@@ -25,7 +26,7 @@
 def kernel(
     nx, ny, ncol, parts,
     ti_hbm, tc_hbm, sp, tp, sm_hbm, tm_hbm, f_out, g_out,
-    ti, tc, tv, cv, sm, tm, X, T0, T1, T2, T3, S, SP, MA, MC, RT, MS, QS, M8, W8, FV, GV, UV, RC, RR, IV,
+    ti, tc, tv, cv, sm, tm, X, T0, T1, T2, T3, S, SP, KA, KB, MA, MC, RT, MS, QS, M8, W8, FV, GV, UV, RC, RR, IV,
     lsem, gs, gr, cr, rs, es,
 ):
     T = (T0, T1, T2, T3)
@@ -37,11 +38,17 @@
     def at(dx, dy):
         return (lax.rem(x + dx + nx, nx) * ny + lax.rem(y + dy + ny, ny), col)
 
-    def row_peer(k):
-        return (lax.rem(row + k, nrow), col)
-
-    def col_peer(k):
-        return (row, lax.rem(col + k, ncol))
+    def hops(d, n):
+        return min(d, n - d)
+
+    row_steps = sorted(
+        ((dx, dy) for dx in range(nx) for dy in range(ny) if dx or dy),
+        key=lambda d: -hops(d[0], nx) - hops(d[1], ny),
+    )
+    row_peers = [at(*d) for d in row_steps]
+    z, core = col // 2, lax.rem(col, 2)
+    col_steps = sorted(((dz, dc) for dz in range(ncol // 2) for dc in range(2) if dz or dc), key=lambda d: -hops(d[0], ncol // 2))
+    col_peers = [(row, lax.rem(z + dz, ncol // 2) * 2 + lax.rem(core + dc, 2)) for dz, dc in col_steps]
 
     tables = [
         pltpu.make_async_copy(a, b, lsem.at[2 + k])
@@ -51,20 +58,25 @@
     ]
     for c in tables:
         c.start()
-    load_x = pltpu.make_async_copy(sp, X, lsem.at[0])
-    load_x.start()
-
-    barrier = pltpu.get_barrier_semaphore()
-    for k in range(1, nrow):
-        pl.semaphore_signal(barrier, inc=1, device_id=row_peer(k), device_id_type=MESH)
-    for k in range(1, ncol):
-        pl.semaphore_signal(barrier, inc=1, device_id=col_peer(k), device_id_type=MESH)
-    pl.semaphore_wait(barrier, nrow + ncol - 2)
-
-    used = []
-
     def rows(dy):
         return pl.ds(pl.multiple_of(lax.rem(y + dy + ny, ny) * 64, 64), 64)
+
+    for b in range(32):
+        pltpu.make_async_copy(tp.at[:, pl.ds(128 * b, 128)], T[0].at[b, rows(0)], lsem.at[1]).start()
+
+    load_x = [pltpu.make_async_copy(sp.at[:, pl.ds(128 * k, 128)], X.at[k], lsem.at[0]) for k in range(8)]
+    for c in load_x:
+        c.start()
+
+    barrier = pltpu.get_barrier_semaphore()
+    greeted = [at(1, 0), at(-1, 0), at(0, 1), at(0, -1)] + col_peers if SHORT else row_peers + col_peers
+    for peer in greeted:
+        pl.semaphore_signal(barrier, inc=1, device_id=peer, device_id_type=MESH)
+    pl.semaphore_wait(barrier, len(greeted))
+
+    mine = T[0].at[:, rows(0)]
+    pltpu.make_async_copy(mine, mine, lsem.at[1]).wait()
+    used = []
 
     steps = {0: (1, 0), 1: (-1, 0), 2: (0, 1), 3: (0, -1)}
 
@@ -86,36 +98,36 @@
     B0, B1 = pl.ds(HALF, QUART), pl.ds(HALF + QUART, QUART)
 
     def own(part):
-        return tp.at[:, part]
+        return T[0].at[part, rows(0)]
 
     def along_y(src, d, part, dy):
-        return tuple(send(src, T[d].at[rows(dy), part], link) for link in (2, 3))
+        return tuple(send(src, T[d].at[part, rows(dy)], link) for link in (2, 3))
 
     def along_x(src, part, dy):
         return (
-            send(src, T[3].at[rows(dy), part], 0),
-            send(src, T[1].at[rows(dy), part], 1),
+            send(src, T[3].at[part, rows(dy)], 0),
+            send(src, T[1].at[part, rows(dy)], 1),
         )
 
     def forward_y(pair, d, low, high):
         k = fresh()
         pair[0].wait_recv()
-        send(T[d].at[rows(-1), low], T[d].at[rows(-1), low], 2, k)
+        send(T[d].at[low, rows(-1)], T[d].at[low, rows(-1)], 2, k)
         pair[1].wait_recv()
-        send(T[d].at[rows(1), high], T[d].at[rows(1), high], 3, k)
+        send(T[d].at[high, rows(1)], T[d].at[high, rows(1)], 3, k)
         return k
 
     def forward_x(pair, dy, low, high):
         k = fresh()
         pair[0].wait_recv()
-        send(T[3].at[rows(dy), low], T[2].at[rows(dy), low], 0, k)
+        send(T[3].at[low, rows(dy)], T[2].at[low, rows(dy)], 0, k)
         pair[1].wait_recv()
-        send(T[1].at[rows(dy), high], T[2].at[rows(dy), high], 1, k)
+        send(T[1].at[high, rows(dy)], T[2].at[high, rows(dy)], 1, k)
         return k
 
     def done(*sems):
         for k in sems:
-            whole = T[0].at[rows(0), A]
+            whole = T[0].at[A, rows(0)]
             pltpu.make_async_copy(whole, whole, gr.at[k]).wait()
 
     scale = LOG2E / math.sqrt(sp.shape[1])
@@ -131,8 +143,8 @@
 
     def product(chunks, t, s):
         here = pl.ds(pl.multiple_of(t * TILE, TILE), TILE)
-        left = [X[here, pl.ds(pl.multiple_of(lax.rem(x + d, nx) * 256, 256), 256)] for d in chunks]
-        right = [T[d][:, pl.ds(ti[s, t] * TILE, TILE)] for d in chunks]
+        left = [X[lax.rem(x + d, nx) * 2 + k, here, :] for d in chunks for k in range(2)]
+        right = [jnp.concatenate([T[d][ti[s, t] * 2 + k] for k in range(2)], axis=1) for d in chunks]
         return jnp.dot(
             jnp.concatenate(left, axis=1), jnp.concatenate(right, axis=0), preferred_element_type=jnp.float32
         ) * scale
@@ -155,8 +167,6 @@
         b1 = along_y(own(B), 0, B, 0)
         ay0 = along_y(own(A), 0, A, 0)
         bx0 = along_x(own(B), B, 0)
-    keep = pltpu.make_async_copy(tp, T[0].at[rows(0), :], lsem.at[1])
-    keep.start()
 
     for c in tables:
         c.wait()
@@ -168,20 +178,19 @@
 
     if parts[0]:
         a2 = forward_x(a1, 0, A0, A1)
-        ay3 = along_y(T[3].at[rows(0), A], 3, A, 0)
-        ay1 = along_y(T[1].at[rows(0), A], 1, A, 0)
+        ay3 = along_y(T[3].at[A, rows(0)], 3, A, 0)
+        ay1 = along_y(T[1].at[A, rows(0)], 1, A, 0)
         b2 = forward_y(b1, 0, B0, B1)
-        bx3 = along_x(T[0].at[rows(-1), B], B, -1)
-        bx1 = along_x(T[0].at[rows(1), B], B, 1)
+        bx3 = along_x(T[0].at[B, rows(-1)], B, -1)
+        bx1 = along_x(T[0].at[B, rows(1)], B, 1)
         fay0 = forward_y(ay0, 0, A0, A1)
         fbx0 = forward_x(bx0, 0, B0, B1)
         done(a2)
-        ay2 = along_y(T[2].at[rows(0), A], 2, A, 0)
+        ay2 = along_y(T[2].at[A, rows(0)], 2, A, 0)
         done(b2)
-        bx2 = along_x(T[0].at[rows(2), B], B, 2)
+        bx2 = along_x(T[0].at[B, rows(2)], B, 2)
         done(fay0)
-    keep.wait()
-    load_x.wait()
+    pltpu.make_async_copy(X, X, lsem.at[0]).wait()
     if parts[1]:
         scores(0)
     if parts[0]:
@@ -197,12 +206,12 @@
     if parts[0]:
         done(fbx0, fbx3, fbx1, fay2, fbx2)
 
-    def give(buf, it, part, me, n, peer, rsem):
-        for k in range(1, n):
+    def give(buf, it, part, me, peers, rsem):
+        for peer in peers:
             pltpu.make_async_remote_copy(
                 src_ref=buf.at[it, part, me], dst_ref=buf.at[it, part, me],
                 send_sem=es.at[0], recv_sem=rsem.at[it, part],
-                device_id=peer(k), device_id_type=MESH,
+                device_id=peer, device_id_type=MESH,
             ).start()
 
     def take(buf, it, part, n, rsem):
@@ -211,7 +220,7 @@
 
     def give_rows(it, half):
         if parts[3]:
-            give(RC, it, half, col, ncol, col_peer, cr)
+            give(RC, it, half, col, col_peers, cr)
 
     def take_rows(it, half):
         if parts[3]:
@@ -219,7 +228,7 @@
 
     def give_columns(it, h):
         if parts[4]:
-            give(RR, it, h, row, nrow, row_peer, rs)
+            give(RR, it, h, row, row_peers, rs)
 
     def take_columns(it, h):
         if parts[4]:
@@ -242,8 +251,7 @@
     def as_column(v):
         return jnp.broadcast_to(v, (128, 128)).T
 
-    def finish(t, to):
-        r = []
+    def finish(t, K):
         for s in range(2):
             p = s * 16 + t
             both = SP[p] + product((2,), t, s)
@@ -251,7 +259,10 @@
                 both = both + idle(t)
             for h in range(2):
                 S[h, p] = both[:, h * 128:(h + 1) * 128]
-                r.append(both[:, h * 128:(h + 1) * 128])
+                K[s, h] = both[:, h * 128:(h + 1) * 128]
+
+    def lane_logs(K, to):
+        r = [K[s, h] for s in range(2) for h in range(2)]
         top = jnp.maximum(jnp.maximum(r[0], r[1]), jnp.maximum(r[2], r[3]))
         e = [jnp.exp2(v - top) for v in r]
         to[...] = top + log2((e[0] + e[1]) + (e[2] + e[3]))
@@ -266,21 +277,26 @@
             QS[h, pl.ds(t, 1), :] = jnp.sum(s8 * jnp.exp2(m8 - top), axis=0, keepdims=True)
 
     if parts[1]:
-        def step(k, carry):
-            finish(2 * k + 1, MC)
-            row_logs(2 * k, MA)
-            finish(2 * k + 2, MA)
-            row_logs(2 * k + 1, MC)
-            return carry
-
-        finish(0, MA)
-        lax.fori_loop(0, 4, step, 0)
+        def stages(t, now):
+            if 2 in now:
+                row_logs(t - 2, MA)
+            if 1 in now:
+                lane_logs(KA, MA)
+            if 0 in now:
+                finish(t, KA)
+
+        def step(t, carry):
+            stages(t, (2, 1, 0))
+            return carry
+
+        stages(0, (0,))
+        stages(1, (1, 0))
+        lax.fori_loop(2, 10, step, 0)
     log_rows(0)
     if parts[1]:
-        lax.fori_loop(4, 7, step, 0)
-        finish(15, MC)
-        row_logs(14, MA)
-        row_logs(15, MC)
+        lax.fori_loop(10, 16, step, 0)
+        stages(16, (2, 1))
+        stages(17, (2,))
     log_rows(1)
 
     def spread(t, to):
@@ -456,10 +472,10 @@
 
     if parts[0]:
         for link in range(4):
-            quarter = X.at[pl.ds(0, 960)]
+            quarter = X.at[pl.ds(0, 2), pl.ds(0, 3840)]
             pltpu.make_async_copy(quarter, quarter, gs.at[link]).wait()
     if parts[3] and parts[4]:
-        sent = X.at[pl.ds(0, 8 * ITERS * (nrow + ncol - 2))]
+        sent = X.at[pl.ds(0, 2), pl.ds(0, 32 * ITERS * (nrow + ncol - 2))]
         pltpu.make_async_copy(sent, sent, es.at[0]).wait()
 
 
@@ -489,10 +505,12 @@
                 pltpu.VMEM(tile_count.shape[::-1], jnp.int32),
                 pltpu.VMEM((n // 128, 128), f32),
                 pltpu.VMEM((m // 128, 128), f32),
-                pltpu.VMEM((n, d), jnp.bfloat16),
-                *[pltpu.VMEM((256, m), jnp.bfloat16) for _ in range(4)],
+                pltpu.VMEM((d // 128, n, 128), jnp.bfloat16),
+                *[pltpu.VMEM((m // 128, 256, 128), jnp.bfloat16) for _ in range(4)],
                 pltpu.VMEM((2, 32, TILE, 128), f32),
                 pltpu.VMEM((32, TILE, TILE), f32),
+                pltpu.VMEM((2, 2, TILE, 128), f32),
+                pltpu.VMEM((2, 2, TILE, 128), f32),
                 pltpu.VMEM((TILE, 128), f32),
                 pltpu.VMEM((TILE, 128), f32),
                 pltpu.VMEM((16, TILE, 128), f32),

time: 98.9 us -> 97.1 us (0.982)
  Pallas kernels: 96.7 us -> 94.8 us
    pallas_call x1, Pallas kernels: 96.7 us -> 94.8 us  [on_device(): pl.pallas_call(functools.partial(kernel, nx, ny, ncol, parts), out_shape=...]
where the time goes in v5:
time: 97.1 us; the launch traced here: 96.8 us
  Pallas kernels  94.8 us (98%)
  other arithmetic  1.35 us (1%)
    pallas_call x1, Pallas kernels, on_device(): pl.pallas_call(functools.partial(kernel, nx, ny, ncol, parts), out_shape=...  94.8 us

profile of v5, /device:TPU:0, one launch (start us, length us, event | category | flops | bytes accessed | tf_op | source)
XLA Modules:
  0.0 96.8 jit_solution(1533791287848530851)
XLA Ops:
  0.6 94.8 %shard_map.77 = (f32[32,128]{1,0:T(8,128)}, f32[32,128]{1,0:T(8,128)}) custom-call(s32[2,16]{1,0:T(2,128)} %bitcast.12, s32[1,16]{1,0:T(1,128)} %bitcast.13, bf16[4096,1024]{1,0:T(8,128)(2,1)} %sp.1, bf16[64,4096]{1,0:T(8,128)(2,1)} %bitcast.9, f32[32,128]{1,0:T(8,128)} %bitcast.10, f32[32,128]{1,0:T(8,128)} %bitcast.11), custom_call_target="tpu_custom_call" | custom-call | tf_op jit(solution)/shard_map/pallas_call | solution.py:493
  95.4 1.4 %multiply_bitcast_fusion = (f32[4096]{0:T(1024)}, f32[4096]{0:T(1024)}) fusion(f32[32,128]{1,0:T(8,128)} %get-tuple-element.5, f32[32,128]{1,0:T(8,128)} %get-tuple-element.4), kind=kLoop, calls=%fused_computation | loop fusion | flops 8192 | bytes 65536 | tf_op jit(solution)/shard_map/reshape | solution.py:541

commit v6 on v5

--- a/solution.py
+++ b/solution.py
@@ -50,6 +50,112 @@
     col_steps = sorted(((dz, dc) for dz in range(ncol // 2) for dc in range(2) if dz or dc), key=lambda d: -hops(d[0], ncol // 2))
     col_peers = [(row, lax.rem(z + dz, ncol // 2) * 2 + lax.rem(core + dc, 2)) for dz, dc in col_steps]
 
+    barrier = pltpu.get_barrier_semaphore()
+    greeted = [at(1, 0), at(-1, 0), at(0, 1), at(0, -1)] + col_peers if SHORT else row_peers + col_peers
+    for peer in greeted:
+        pl.semaphore_signal(barrier, inc=1, device_id=peer, device_id_type=MESH)
+    def rows(dy):
+        return pl.ds(pl.multiple_of(lax.rem(y + dy + ny, ny) * 64, 64), 64)
+
+    for b in range(32):
+        pltpu.make_async_copy(tp.at[:, pl.ds(128 * b, 128)], T[0].at[b, rows(0)], lsem.at[1]).start()
+
+    pl.semaphore_wait(barrier, len(greeted))
+
+    mine = T[0].at[:, rows(0)]
+    pltpu.make_async_copy(mine, mine, lsem.at[1]).wait()
+    used = []
+
+    steps = {0: (1, 0), 1: (-1, 0), 2: (0, 1), 3: (0, -1)}
+
+    def fresh():
+        used.append(0)
+        return len(used) - 1
+
+    def send(src, dst, link, k=None):
+        k = fresh() if k is None else k
+        c = pltpu.make_async_remote_copy(
+            src_ref=src, dst_ref=dst, send_sem=gs.at[link], recv_sem=gr.at[k],
+            device_id=at(*steps[link]), device_id_type=MESH,
+        )
+        c.start()
+        return c
+
+    A, B = pl.ds(0, HALF), pl.ds(HALF, HALF)
+    A0, A1 = pl.ds(0, QUART), pl.ds(QUART, QUART)
+    B0, B1 = pl.ds(HALF, QUART), pl.ds(HALF + QUART, QUART)
+
+    def own(part):
+        return T[0].at[part, rows(0)]
+
+    def along_y(src, d, part, dy):
+        return tuple(send(src, T[d].at[part, rows(dy)], link) for link in (2, 3))
+
+    def along_x(src, part, dy):
+        return (
+            send(src, T[3].at[part, rows(dy)], 0),
+            send(src, T[1].at[part, rows(dy)], 1),
+        )
+
+    def forward_y(pair, d, low, high):
+        k = fresh()
+        pair[0].wait_recv()
+        send(T[d].at[low, rows(-1)], T[d].at[low, rows(-1)], 2, k)
+        pair[1].wait_recv()
+        send(T[d].at[high, rows(1)], T[d].at[high, rows(1)], 3, k)
+        return k
+
+    def forward_x(pair, dy, low, high):
+        k = fresh()
+        pair[0].wait_recv()
+        send(T[3].at[low, rows(dy)], T[2].at[low, rows(dy)], 0, k)
+        pair[1].wait_recv()
+        send(T[1].at[high, rows(dy)], T[2].at[high, rows(dy)], 1, k)
+        return k
+
+    def done(*sems):
+        for k in sems:
+            whole = T[0].at[A, rows(0)]
+            pltpu.make_async_copy(whole, whole, gr.at[k]).wait()
+
+    scale = LOG2E / math.sqrt(sp.shape[1])
+    wide = (32, 8, 128)
+
+    def fold(op, v):
+        v = v.reshape((v.shape[0] // 4, 4) + v.shape[1:])
+        v = functools.reduce(op, [v[k] for k in range(v.shape[0])])
+        while v.shape[0] > 1:
+            n = v.shape[0] // 2
+            v = op(v[:n], v[n:])
+        return v[0]
+
+    def product(chunks, t, s):
+        here = pl.ds(pl.multiple_of(t * TILE, TILE), TILE)
+        left = [X[lax.rem(x + d, nx) * 2 + k, here, :] for d in chunks for k in range(2)]
+        right = [jnp.concatenate([T[d][ti[s, t] * 2 + k] for k in range(2)], axis=1) for d in chunks]
+        return jnp.dot(
+            jnp.concatenate(left, axis=1), jnp.concatenate(right, axis=0), preferred_element_type=jnp.float32
+        ) * scale
+
+    def scores(*chunks):
+        def body(t, carry):
+            for s in range(2):
+                p = s * 16 + t
+                new = product(chunks, t, s)
+                SP[p] = new if chunks == (0,) else SP[p] + new
+            return carry
+
+        lax.fori_loop(0, 16, body, 0)
+
+    def idle(t):
+        return (tc[0, t].astype(jnp.float32) - 2.0) * 1e30
+
+    if parts[0]:
+        a1 = along_x(own(A), A, 0)
+        b1 = along_y(own(B), 0, B, 0)
+        ay0 = along_y(own(A), 0, A, 0)
+        bx0 = along_x(own(B), B, 0)
+
     tables = [
         pltpu.make_async_copy(a, b, lsem.at[2 + k])
         for k, (a, b) in enumerate(
@@ -58,115 +164,9 @@
     ]
     for c in tables:
         c.start()
-    def rows(dy):
-        return pl.ds(pl.multiple_of(lax.rem(y + dy + ny, ny) * 64, 64), 64)
-
-    for b in range(32):
-        pltpu.make_async_copy(tp.at[:, pl.ds(128 * b, 128)], T[0].at[b, rows(0)], lsem.at[1]).start()
-
     load_x = [pltpu.make_async_copy(sp.at[:, pl.ds(128 * k, 128)], X.at[k], lsem.at[0]) for k in range(8)]
     for c in load_x:
         c.start()
-
-    barrier = pltpu.get_barrier_semaphore()
-    greeted = [at(1, 0), at(-1, 0), at(0, 1), at(0, -1)] + col_peers if SHORT else row_peers + col_peers
-    for peer in greeted:
-        pl.semaphore_signal(barrier, inc=1, device_id=peer, device_id_type=MESH)
-    pl.semaphore_wait(barrier, len(greeted))
-
-    mine = T[0].at[:, rows(0)]
-    pltpu.make_async_copy(mine, mine, lsem.at[1]).wait()
-    used = []
-
-    steps = {0: (1, 0), 1: (-1, 0), 2: (0, 1), 3: (0, -1)}
-
-    def fresh():
-        used.append(0)
-        return len(used) - 1
-
-    def send(src, dst, link, k=None):
-        k = fresh() if k is None else k
-        c = pltpu.make_async_remote_copy(
-            src_ref=src, dst_ref=dst, send_sem=gs.at[link], recv_sem=gr.at[k],
-            device_id=at(*steps[link]), device_id_type=MESH,
-        )
-        c.start()
-        return c
-
-    A, B = pl.ds(0, HALF), pl.ds(HALF, HALF)
-    A0, A1 = pl.ds(0, QUART), pl.ds(QUART, QUART)
-    B0, B1 = pl.ds(HALF, QUART), pl.ds(HALF + QUART, QUART)
-
-    def own(part):
-        return T[0].at[part, rows(0)]
-
-    def along_y(src, d, part, dy):
-        return tuple(send(src, T[d].at[part, rows(dy)], link) for link in (2, 3))
-
-    def along_x(src, part, dy):
-        return (
-            send(src, T[3].at[part, rows(dy)], 0),
-            send(src, T[1].at[part, rows(dy)], 1),
-        )
-
-    def forward_y(pair, d, low, high):
-        k = fresh()
-        pair[0].wait_recv()
-        send(T[d].at[low, rows(-1)], T[d].at[low, rows(-1)], 2, k)
-        pair[1].wait_recv()
-        send(T[d].at[high, rows(1)], T[d].at[high, rows(1)], 3, k)
-        return k
-
-    def forward_x(pair, dy, low, high):
-        k = fresh()
-        pair[0].wait_recv()
-        send(T[3].at[low, rows(dy)], T[2].at[low, rows(dy)], 0, k)
-        pair[1].wait_recv()
-        send(T[1].at[high, rows(dy)], T[2].at[high, rows(dy)], 1, k)
-        return k
-
-    def done(*sems):
-        for k in sems:
-            whole = T[0].at[A, rows(0)]
-            pltpu.make_async_copy(whole, whole, gr.at[k]).wait()
-
-    scale = LOG2E / math.sqrt(sp.shape[1])
-    wide = (32, 8, 128)
-
-    def fold(op, v):
-        v = v.reshape((v.shape[0] // 4, 4) + v.shape[1:])
-        v = functools.reduce(op, [v[k] for k in range(v.shape[0])])
-        while v.shape[0] > 1:
-            n = v.shape[0] // 2
-            v = op(v[:n], v[n:])
-        return v[0]
-
-    def product(chunks, t, s):
-        here = pl.ds(pl.multiple_of(t * TILE, TILE), TILE)
-        left = [X[lax.rem(x + d, nx) * 2 + k, here, :] for d in chunks for k in range(2)]
-        right = [jnp.concatenate([T[d][ti[s, t] * 2 + k] for k in range(2)], axis=1) for d in chunks]
-        return jnp.dot(
-            jnp.concatenate(left, axis=1), jnp.concatenate(right, axis=0), preferred_element_type=jnp.float32
-        ) * scale
-
-    def scores(*chunks):
-        def body(t, carry):
-            for s in range(2):
-                p = s * 16 + t
-                new = product(chunks, t, s)
-                SP[p] = new if chunks == (0,) else SP[p] + new
-            return carry
-
-        lax.fori_loop(0, 16, body, 0)
-
-    def idle(t):
-        return (tc[0, t].astype(jnp.float32) - 2.0) * 1e30
-
-    if parts[0]:
-        a1 = along_x(own(A), A, 0)
-        b1 = along_y(own(B), 0, B, 0)
-        ay0 = along_y(own(A), 0, A, 0)
-        bx0 = along_x(own(B), B, 0)
 
     for c in tables:
         c.wait()
@@ -318,7 +318,7 @@
                 RT[t + 1] = MC[...]
             return carry
 
-        lax.fori_loop(0, 4, body, 0)
+        lax.fori_loop(0, 4, body, 0, unroll=2)
 
     def each_kept(visit):
         def body(k, carry):
@@ -362,7 +362,7 @@
                 RC[it, half, col, h, pl.ds(k, 1), :] = over_lanes(jnp.add, total[h * 128:(h + 1) * 128])
             return carry
 
-        lax.fori_loop(0, 8, step, 0, unroll=2)
+        lax.fori_loop(0, 8, step, 0, unroll=8)
         give_rows(it, half)
 
     def column_sums(t, by, lanes):
@@ -425,7 +425,7 @@
                     W8[h, p] = W8[h, p] * UV[h, pl.ds(ti[s, t], 1), :]
             return carry
 
-        lax.fori_loop(0, 16, body, 0, unroll=8)
+        lax.fori_loop(0, 16, body, 0, unroll=16)
 
     def columns_arrive(it, h):
         take_columns(it, h)

time: 97.1 us -> 95.8 us (0.987)
  Pallas kernels: 94.8 us -> 93.5 us
    pallas_call x1, Pallas kernels: 94.8 us -> 93.5 us  [on_device(): pl.pallas_call(functools.partial(kernel, nx, ny, ncol, parts), out_shape=...]
where the time goes in v6:
time: 95.8 us; the launch traced here: 95.5 us
  Pallas kernels  93.5 us (98%)
  other arithmetic  1.35 us (1%)
    pallas_call x1, Pallas kernels, on_device(): pl.pallas_call(functools.partial(kernel, nx, ny, ncol, parts), out_shape=...  93.5 us

profile of v6, /device:TPU:0, one launch (start us, length us, event | category | flops | bytes accessed | tf_op | source)
XLA Modules:
  0.0 95.5 jit_solution(6701468377579439162)
XLA Ops:
  0.6 93.5 %shard_map.77 = (f32[32,128]{1,0:T(8,128)}, f32[32,128]{1,0:T(8,128)}) custom-call(s32[2,16]{1,0:T(2,128)} %bitcast.12, s32[1,16]{1,0:T(1,128)} %bitcast.13, bf16[4096,1024]{1,0:T(8,128)(2,1)} %sp.1, bf16[64,4096]{1,0:T(8,128)(2,1)} %bitcast.9, f32[32,128]{1,0:T(8,128)} %bitcast.10, f32[32,128]{1,0:T(8,128)} %bitcast.11), custom_call_target="tpu_custom_call" | custom-call | tf_op jit(solution)/shard_map/pallas_call | solution.py:493
  94.2 1.4 %multiply_bitcast_fusion = (f32[4096]{0:T(1024)}, f32[4096]{0:T(1024)}) fusion(f32[32,128]{1,0:T(8,128)} %get-tuple-element.5, f32[32,128]{1,0:T(8,128)} %get-tuple-element.4), kind=kLoop, calls=%fused_computation | loop fusion | flops 8192 | bytes 65536 | tf_op jit(solution)/shard_map/reshape | solution.py:541

commit v7 on v6

--- a/solution.py
+++ b/solution.py
@@ -145,7 +145,7 @@
                 SP[p] = new if chunks == (0,) else SP[p] + new
             return carry
 
-        lax.fori_loop(0, 16, body, 0)
+        lax.fori_loop(0, 16, body, 0, unroll=2)
 
     def idle(t):
         return (tc[0, t].astype(jnp.float32) - 2.0) * 1e30
@@ -325,7 +325,7 @@
             visit(8 + k, RT.at[8 + k])
             return carry
 
-        lax.fori_loop(0, 8, body, 0, unroll=2)
+        lax.fori_loop(0, 8, body, 0, unroll=4)
 
     def block(p, h):
         return S[h, p].reshape(wide)

time: 95.8 us -> 93.8 us (0.979)
  Pallas kernels: 93.5 us -> 91.2 us
    pallas_call x1, Pallas kernels: 93.5 us -> 91.2 us  [on_device(): pl.pallas_call(functools.partial(kernel, nx, ny, ncol, parts), out_shape=...]
where the time goes in v7:
time: 93.8 us; the launch traced here: 93.2 us
  Pallas kernels  91.2 us (97%)
  other arithmetic  1.35 us (1%)
    pallas_call x1, Pallas kernels, on_device(): pl.pallas_call(functools.partial(kernel, nx, ny, ncol, parts), out_shape=...  91.2 us

profile of v7, /device:TPU:0, one launch (start us, length us, event | category | flops | bytes accessed | tf_op | source)
XLA Modules:
  0.0 93.2 jit_solution(17711252229136053184)
XLA Ops:
  0.6 91.2 %shard_map.77 = (f32[32,128]{1,0:T(8,128)}, f32[32,128]{1,0:T(8,128)}) custom-call(s32[2,16]{1,0:T(2,128)} %bitcast.12, s32[1,16]{1,0:T(1,128)} %bitcast.13, bf16[4096,1024]{1,0:T(8,128)(2,1)} %sp.1, bf16[64,4096]{1,0:T(8,128)(2,1)} %bitcast.9, f32[32,128]{1,0:T(8,128)} %bitcast.10, f32[32,128]{1,0:T(8,128)} %bitcast.11), custom_call_target="tpu_custom_call" | custom-call | tf_op jit(solution)/shard_map/pallas_call | solution.py:493
  91.9 1.4 %multiply_bitcast_fusion = (f32[4096]{0:T(1024)}, f32[4096]{0:T(1024)}) fusion(f32[32,128]{1,0:T(8,128)} %get-tuple-element.5, f32[32,128]{1,0:T(8,128)} %get-tuple-element.4), kind=kLoop, calls=%fused_computation | loop fusion | flops 8192 | bytes 65536 | tf_op jit(solution)/shard_map/reshape | solution.py:541
